TPU v7x, 512 devices: a whole 4x4x16 slice. The times are simulated.
512 devices in a mesh: visit: 32 (over z, x_lo), patch: 16 (over x_hi, y, core).
Axes of the slice: x: 4 (x_hi: 2, x_lo: 2; x = x_hi * 2 + x_lo), y: 4, z: 16, core: 2. Of those that a mesh axis runs over, the one named last changes fastest.
Arguments:
- templates: float32 [32, 2, 256, 1024], P('visit', None, 'patch'), may hold values from -16 to 16, as said below
- owners: int32 [2], replicated, may hold values from 0 to 31, as said below
- science: float32 [2, 32, 256, 1024], P(None, 'visit', 'patch'), may hold values from -40 to 40
- sci_var: float32 [2, 32, 256, 1024], P(None, 'visit', 'patch'), may hold values from 0.03 to 0.3
- bad_pixels: int32 [2, 32, 256, 1024], P(None, 'visit', 'patch'), may hold values 0 or 1
Outputs:
- significance: float32 [2, 32, 256, 1024], P(None, 'visit', 'patch')
Inputs may be any that keep to these rules, and one draw needn't show every extreme that they name: `owners`: the steps' entries are distinct indices of stored tiles, one of them always 32 - 1. `templates`: variances (index 1) lie in 0.01 to 0.1.
All inputs are finite; a program needn't handle non-finite values. No bound on the sum of `bad_pixels` on one device may be relied on, other than what follows from the above.
Results may differ from a plain program's by a relative error of at most 0.0003.
Values sent between devices are 32-bit elements; how exact they have to be, the bound alone decides.
A program may use at most 64 MiB of HBM per device.

v0:
```python
import jax
import jax.numpy as jnp
import numpy as np
from jax import lax
from jax.sharding import PartitionSpec as P

NPROF = 5
RAD = 10
STEPS = 2


ridge = 1.0


def from_root(block, axis, holder):
    block = jnp.where(lax.axis_index(axis) == holder, block, jnp.zeros_like(block))
    return lax.psum(block, axis)


def padded(cells, sides, width):
    for axis, dim in sides:
        count = lax.axis_size(axis)
        ends = count - 1
        head = lax.slice_in_dim(cells, 0, width, axis=dim)
        tail = lax.slice_in_dim(cells, cells.shape[dim] - width, cells.shape[dim], axis=dim)
        cells = jnp.concatenate(
            [
                lax.ppermute(tail, axis, [(i, (i + 1) % count) for i in range(ends)]),
                cells,
                lax.ppermute(head, axis, [((i + 1) % count, i) for i in range(ends)]),
            ],
            axis=dim,
        )
    return cells


def profile_table():
    offsets = np.arange(-RAD, RAD + 1) * 1.0
    recipe = [(1.0, 0), (1.5, 1), (2.0, 2), (3.0, 0), (4.0, 1)]
    profiles = []
    for spread, degree in recipe[:NPROF]:
        profile = offsets**degree * np.exp(-offsets * offsets / (2.0 * spread * spread))
        for earlier in profiles:
            profile = profile - np.dot(earlier, profile) * earlier
        profile = profile / np.sqrt(np.dot(profile, profile))
        profiles.append(profile)
    return np.stack(profiles)


def band_table(profiles, outputs, inputs):
    distance = jnp.arange(inputs)[None, :] - jnp.arange(outputs)[:, None]
    table = jnp.zeros((NPROF, outputs, inputs), jnp.float32)
    for offset in range(2 * RAD + 1):
        table = (
            table + profiles[:, offset, None, None] * (distance == offset).astype(jnp.float32)[None]
        )
    return table


def basis_images(extended):
    profiles = jnp.asarray(profile_table(), jnp.float32)
    height = extended.shape[0] - 2 * RAD
    across = extended.shape[1]
    block_width = 128
    block_count = across // block_width
    widened = jnp.pad(extended, ((0, 0), (RAD, RAD)))
    blocks = jnp.stack(
        [
            widened[:, start * block_width : start * block_width + block_width + 2 * RAD]
            for start in range(block_count)
        ]
    )
    col_table = jnp.transpose(band_table(profiles, block_width, block_width + 2 * RAD), (0, 2, 1))
    columns = jnp.einsum("srx,kxc->krsc", blocks, col_table, precision=lax.Precision.HIGHEST)
    columns = columns.reshape(NPROF, extended.shape[0], across)
    row_table = band_table(profiles, height, height + 2 * RAD)
    images = jnp.einsum("lhr,krc->klhc", row_table, columns, precision=lax.Precision.HIGHEST)
    return images.reshape(NPROF * NPROF, height, across)


def solve_kernel(normal_mat, normal_rhs):
    count = normal_mat.shape[0]
    factor = jnp.linalg.cholesky(normal_mat + ridge * jnp.eye(count, dtype=jnp.float32))
    return jax.scipy.linalg.cho_solve((factor, True), normal_rhs)


def finish_step(normal_mat, normal_rhs, flattened, usable, noise_var, image_sci):
    kernel_coef = jax.vmap(solve_kernel)(normal_mat, normal_rhs)
    fitted = jnp.einsum(
        "vb,bp->vp", kernel_coef, flattened, precision=lax.Precision.HIGHEST
    ).reshape(image_sci.shape)
    return usable * (image_sci - fitted) / jnp.sqrt(noise_var)


def shards(templates, owners, science, sci_var, bad_pixels):
    own_pair = templates[0]
    visit_count = science.shape[1]
    basis_count = NPROF * NPROF
    results = []
    for current in range(STEPS):
        owner_index = owners[current]
        arrived = from_root(own_pair, "visit", owner_index)
        extended = padded(arrived[0], (("patch", 0),), RAD)
        tile_var = arrived[1]
        images = basis_images(extended)
        flattened = images.reshape(basis_count, -1)
        usable = (1 - bad_pixels[current]).astype(jnp.float32)
        noise_var = sci_var[current] + tile_var[None]
        weight = usable / noise_var
        weighted = (images[None] * weight[:, None]).reshape(visit_count, basis_count, -1)
        normal_mat = jnp.einsum("vbp,cp->vbc", weighted, flattened, precision=lax.Precision.HIGHEST)
        normal_rhs = jnp.einsum(
            "cp,vp->vc",
            flattened,
            (weight * science[current]).reshape(visit_count, -1),
            precision=lax.Precision.HIGHEST,
        )
        summed_mat, summed_rhs = lax.psum((normal_mat, normal_rhs), "patch")
        results.append(
            finish_step(summed_mat, summed_rhs, flattened, usable, noise_var, science[current])
        )
    return jnp.stack(results)


def solution(mesh):
    return jax.shard_map(
        shards,
        mesh=mesh,
        in_specs=(
            P("visit", None, "patch", None),
            P(),
            P(None, "visit", "patch", None),
            P(None, "visit", "patch", None),
            P(None, "visit", "patch", None),
        ),
        out_specs=P(None, "visit", "patch", None),
        check_vma=False,
    )
```

profile of v0, /device:TPU:4, one launch (start us, length us, event | category | flops | bytes accessed | tf_op | source)
XLA Modules:
  0.0 429.1 jit_solution(2009927834076208268)
XLA Ops:
  6.8 1.4 fusion.136
  9.5 1.6 select_bitcast_fusion.1
  12.7 263.9 %all-reduce.6.cloned.1.call-done = (f32[2,16,1024]{2,1,0:T(8,128)}, f32[2,16,1024]{2,1,0:T(8,128)}) async-done(((f32[2,16,1024]{2,1,0:T(8,128)}, f32[2,16,1024]{2,1,0:T(8,128)}), (f32[2,16,1024]{2,1,0:T(8,128)}, f32[2,16,1024]{2,1,0:T(8,128)})) %all-reduce.6.cloned.1.call-update) | async-done | bytes 262160 | tf_op jit(solution)/shard_map/psum | solution.py:17
  277.5 1.9 collective-permute-start.2
  279.5 7.3 %collective-permute-start.3 = (f32[10,1024]{1,0:T(8,128)S(1)}, f32[10,1024]{1,0:T(8,128)S(1)}, u32[]{:S(2)}, u32[]{:S(2)}) collective-permute-start(f32[10,1024]{1,0:T(8,128)S(1)} %get-tuple-element.24), channel_id=1, source_target_pairs={{1,0},{2,1},{3,2},{4,3},{5,4},{6,5},{7,6},{8,7},{9,8},{10,9},{11,1... | collective-permute-start | bytes 122888 | tf_op jit(solution)/shard_map/ppermute | solution.py:30
  287.6 1.9 collective-permute-start
  289.6 7.3 %collective-permute-start.1 = (f32[10,1024]{1,0:T(8,128)S(1)}, f32[10,1024]{1,0:T(8,128)S(1)}, u32[]{:S(2)}, u32[]{:S(2)}) collective-permute-start(f32[10,1024]{1,0:T(8,128)S(1)} %get-tuple-element.22), channel_id=1, source_target_pairs={{1,0},{2,1},{3,2},{4,3},{5,4},{6,5},{7,6},{8,7},{9,8},{10,9},{11,1... | collective-permute-start | bytes 122888 | tf_op jit(solution)/shard_map/ppermute | solution.py:30
  303.1 1.6 bitcast_multiply_fusion.1
  305.0 1.6 bitcast_multiply_fusion
  309.7 1.8 convolution_bitcast_fusion.3
  311.6 2.5 fusion.137
  316.8 2.4 convolution_bitcast_fusion.2
  319.3 2.3 fusion.138
  321.6 70.9 %all-reduce.3 = (f32[1,25,25]{1,2,0:T(8,128)}, f32[1,25]{1,0:T(1,128)}, f32[1,25,25]{1,2,0:T(8,128)}, f32[1,25]{1,0:T(1,128)}) all-reduce(f32[1,25,25]{1,2,0:T(8,128)} %convolution_bitcast_fusion.2, f32[1,25]{1,0:T(1,128)} %fusion.138, ...), channel_id=1, replica_groups=mesh['visit'=32,'patch'=16] {'patch'}, use_global_device_ids=true, to_apply=%region_6.9 | all-reduce | flops 1300 | bytes 10400 | tf_op jit(solution)/shard_map/psum | solution.py:118
  392.5 1.3 convert_add_fusion
  394.6 1.3 fusion.86
  396.0 3.0 custom-call.12
  400.8 2.6 custom-call.13
  404.9 1.3 convert_add_fusion.1
  407.0 1.3 fusion.89
  408.3 3.0 custom-call.10
  413.3 2.6 custom-call.11
  416.9 2.6 fusion
  419.5 2.0 fusion.2
  (140 shorter events, 24.1 us)
Async XLA Ops:
  6.5 5.0 %copy-start.9 = (f32[5]{0:T(128)S(1)}, f32[5]{0:T(128)}, u32[]{:S(2)}) copy-start(f32[5]{0:T(128)} %constant.161) | copy-start | bytes 64
  6.5 5.0 %copy-start.10 = (f32[5]{0:T(128)S(1)}, f32[5]{0:T(128)}, u32[]{:S(2)}) copy-start(f32[5]{0:T(128)} %constant.159) | copy-start | bytes 64
  6.5 5.1 %copy-start.11 = (f32[5]{0:T(128)S(1)}, f32[5]{0:T(128)}, u32[]{:S(2)}) copy-start(f32[5]{0:T(128)} %constant.157) | copy-start | bytes 64
  6.5 5.1 %copy-start.12 = (f32[5]{0:T(128)S(1)}, f32[5]{0:T(128)}, u32[]{:S(2)}) copy-start(f32[5]{0:T(128)} %constant.155) | copy-start | bytes 64
  6.6 5.1 %copy-start.13 = (f32[5]{0:T(128)S(1)}, f32[5]{0:T(128)}, u32[]{:S(2)}) copy-start(f32[5]{0:T(128)} %constant.153) | copy-start | bytes 64
  6.6 5.1 %copy-start.14 = (f32[5]{0:T(128)S(1)}, f32[5]{0:T(128)}, u32[]{:S(2)}) copy-start(f32[5]{0:T(128)} %constant.151) | copy-start | bytes 64
  6.6 5.1 %copy-start.15 = (f32[5]{0:T(128)S(1)}, f32[5]{0:T(128)}, u32[]{:S(2)}) copy-start(f32[5]{0:T(128)} %constant.149) | copy-start | bytes 64
  6.6 5.1 %copy-start.16 = (f32[5]{0:T(128)S(1)}, f32[5]{0:T(128)}, u32[]{:S(2)}) copy-start(f32[5]{0:T(128)} %constant.147) | copy-start | bytes 64
  6.6 5.1 %copy-start.17 = (f32[5]{0:T(128)S(1)}, f32[5]{0:T(128)}, u32[]{:S(2)}) copy-start(f32[5]{0:T(128)} %constant.145) | copy-start | bytes 64
  6.6 5.1 %copy-start.18 = (f32[5]{0:T(128)S(1)}, f32[5]{0:T(128)}, u32[]{:S(2)}) copy-start(f32[5]{0:T(128)} %constant.143) | copy-start | bytes 64
  6.6 5.1 %copy-start.19 = (f32[5]{0:T(128)S(1)}, f32[5]{0:T(128)}, u32[]{:S(2)}) copy-start(f32[5]{0:T(128)} %constant.141) | copy-start | bytes 64
  6.6 5.0 %copy-start.20 = (f32[5]{0:T(128)S(1)}, f32[5]{0:T(128)}, u32[]{:S(2)}) copy-start(f32[5]{0:T(128)} %constant.139) | copy-start | bytes 64
  6.7 5.0 %copy-start.21 = (f32[5]{0:T(128)S(1)}, f32[5]{0:T(128)}, u32[]{:S(2)}) copy-start(f32[5]{0:T(128)} %constant.137) | copy-start | bytes 64
  6.7 5.0 %copy-start.22 = (f32[5]{0:T(128)S(1)}, f32[5]{0:T(128)}, u32[]{:S(2)}) copy-start(f32[5]{0:T(128)} %constant.135) | copy-start | bytes 64
  6.7 5.0 %copy-start.23 = (f32[5]{0:T(128)S(1)}, f32[5]{0:T(128)}, u32[]{:S(2)}) copy-start(f32[5]{0:T(128)} %constant.133) | copy-start | bytes 64
  6.7 5.0 %copy-start.24 = (f32[5]{0:T(128)S(1)}, f32[5]{0:T(128)}, u32[]{:S(2)}) copy-start(f32[5]{0:T(128)} %constant.131) | copy-start | bytes 64
  6.8 269.8 %all-reduce.6.cloned.1.call-start = ((), (), s32[]{:S(2)}) async-start(), calls=%async_computation | async-start | bytes 524288 | tf_op jit(solution)/shard_map/psum | solution.py:17
  11.3 285.5 %copy-start.2 = (f32[2,1,16,1024]{3,2,1,0:T(8,128)S(1)}, f32[2,1,16,1024]{3,2,1,0:T(8,128)}, u32[]{:S(2)}) copy-start(f32[2,1,16,1024]{3,2,1,0:T(8,128)} %param.12) | copy-start | bytes 393220
  11.3 285.5 %copy-start.3 = (f32[2,1,16,1024]{3,2,1,0:T(8,128)S(1)}, f32[2,1,16,1024]{3,2,1,0:T(8,128)}, u32[]{:S(2)}) copy-start(f32[2,1,16,1024]{3,2,1,0:T(8,128)} %param.13) | copy-start | bytes 393220
  11.3 285.5 %copy-start.4 = (s32[2,1,16,1024]{3,2,1,0:T(8,128)S(1)}, s32[2,1,16,1024]{3,2,1,0:T(8,128)}, u32[]{:S(2)}) copy-start(s32[2,1,16,1024]{3,2,1,0:T(8,128)} %param.14) | copy-start | bytes 393220
  277.5 21.7 %collective-permute-start.2 = (f32[10,1024]{1,0:T(8,128)S(1)}, f32[10,1024]{1,0:T(8,128)S(1)}, u32[]{:S(2)}, u32[]{:S(2)}) collective-permute-start(f32[10,1024]{1,0:T(8,128)S(1)} %get-tuple-element.23), channel_id=1, source_target_pairs={{0,1},{1,2},{2,3},{3,4},{4,5},{5,6},{6,7},{7,8},{8,9},{9,10},{10,1... | collective-permute-start | bytes 122888 | tf_op jit(solution)/shard_map/ppermute | solution.py:28
  279.5 19.8 %collective-permute-start.3 = (f32[10,1024]{1,0:T(8,128)S(1)}, f32[10,1024]{1,0:T(8,128)S(1)}, u32[]{:S(2)}, u32[]{:S(2)}) collective-permute-start(f32[10,1024]{1,0:T(8,128)S(1)} %get-tuple-element.24), channel_id=1, source_target_pairs={{1,0},{2,1},{3,2},{4,3},{5,4},{6,5},{7,6},{8,7},{9,8},{10,9},{11,1... | collective-permute-start | bytes 122888 | tf_op jit(solution)/shard_map/ppermute | solution.py:30
  287.6 11.6 %collective-permute-start = (f32[10,1024]{1,0:T(8,128)S(1)}, f32[10,1024]{1,0:T(8,128)S(1)}, u32[]{:S(2)}, u32[]{:S(2)}) collective-permute-start(f32[10,1024]{1,0:T(8,128)S(1)} %get-tuple-element.21), channel_id=1, source_target_pairs={{0,1},{1,2},{2,3},{3,4},{4,5},{5,6},{6,7},{7,8},{8,9},{9,10},{10,1... | collective-permute-start | bytes 122888 | tf_op jit(solution)/shard_map/ppermute | solution.py:28
  289.6 9.7 %collective-permute-start.1 = (f32[10,1024]{1,0:T(8,128)S(1)}, f32[10,1024]{1,0:T(8,128)S(1)}, u32[]{:S(2)}, u32[]{:S(2)}) collective-permute-start(f32[10,1024]{1,0:T(8,128)S(1)} %get-tuple-element.22), channel_id=1, source_target_pairs={{1,0},{2,1},{3,2},{4,3},{5,4},{6,5},{7,6},{8,7},{9,8},{10,9},{11,1... | collective-permute-start | bytes 122888 | tf_op jit(solution)/shard_map/ppermute | solution.py:30
  (10 other events, 43.4 us)
Sparse Core Ops, SparseCore 0:
  11.2 265.3 all-reduce.5
where the time goes:
time: 430 us; the launch traced here: 429 us
  waiting for transfers between devices  264 us (61%)
  blocking collectives  70.9 us (16%)
  other arithmetic  24.9 us (6%)
  matrix products  21.2 us (5%)
  starting transfers between devices  18.4 us (4%)
  between operations  15.5 us (4%)
  local copies, waits for them, and re-layouts  14.3 us (3%)
    psum x1, waiting for transfers between devices, from_root(): return lax.psum(block, axis)  264 us
    psum x1, blocking collectives, shards(): summed_mat, summed_rhs = lax.psum((normal_mat, normal_rhs), 'patch')  70.9 us
    ppermute x2, starting transfers between devices, padded(): lax.ppermute(head, axis, [((i + 1) % count, i) for i in range(ends)])  14.5 us
  transfers between devices with their start and end apart: 5, of which 1 were waited for; matrix products, arithmetic and copies ran while one was open for 1% of the time, Pallas kernels for 0%

commit v1 on v0

v1 whole, which is shorter than its diff:
```python
import functools

import jax
import jax.numpy as jnp
import ml_dtypes
import numpy as np
from jax import lax
from jax.experimental import pallas as pl
from jax.experimental.pallas import tpu as pltpu
from jax.sharding import PartitionSpec as P

NPROF = 5
RAD = 10
STEPS = 2
RIDGE = 1.0

GROUP = 8
NGROUPS = 4
NPATCH = 16
SLOT = 7
FIXED = 31
ROWS = 16
LANES = 128
NBLOCKS = 8
SCI = 5
MESH = pl.DeviceIdType.MESH

PARTS = (
    (0, 1, 6, 7, 0),
    (1, 1, 13, 3, 0),
    (1, 0, 0, 3, 3),
    (2, 0, 3, 7, 0),
    (3, 0, 10, 6, 0),
    (4, -1, 0, 7, 0),
    (5, -1, 7, 3, 0),
    (5, 0, 16, 3, 4),
    (6, 0, 19, 7, 0),
    (7, 0, 26, 6, 0),
)
VAR_AT = 39
POSITIONS = 40


def image_positions():
    return list(range(0, 13)) + list(range(14, 27)) + list(range(28, 38))


def profile_table():
    offsets = np.arange(-RAD, RAD + 1) * 1.0
    recipe = [(1.0, 0), (1.5, 1), (2.0, 2), (3.0, 0), (4.0, 1)]
    profiles = []
    for spread, degree in recipe[:NPROF]:
        profile = offsets**degree * np.exp(-offsets * offsets / (2.0 * spread * spread))
        for earlier in profiles:
            profile = profile - np.dot(earlier, profile) * earlier
        profile = profile / np.sqrt(np.dot(profile, profile))
        profiles.append(profile)
    return np.stack(profiles)


def column_table():
    prof = profile_table().astype(np.float32)
    table = np.zeros((2 * LANES, NPROF * LANES), np.float32)
    for k in range(NPROF):
        for n in range(LANES):
            first = n + LANES // 2 - RAD
            table[first : first + 2 * RAD + 1, k * LANES + n] = prof[k]
    return table


def split3(x):
    high = x.astype(ml_dtypes.bfloat16).astype(np.float32)
    mid = (x - high).astype(ml_dtypes.bfloat16).astype(np.float32)
    low = (x - high - mid).astype(ml_dtypes.bfloat16).astype(np.float32)
    return high, mid, low


def row_table():
    prof = profile_table().astype(np.float32)
    places = image_positions()
    table = np.zeros((ROWS * 8, POSITIONS), np.float32)
    for h in range(ROWS):
        for l in range(NPROF):
            for a in range(2 * RAD + 1):
                table[h * 8 + l, places[h + a]] = prof[l, a]
    high, mid, low = split3(table)
    return np.concatenate([high, high, high, mid, mid, low], axis=1).astype(ml_dtypes.bfloat16)


def rounded(x):
    return x.astype(jnp.bfloat16).astype(jnp.float32)


def normal_part(slot, step, ag, ag_flat, cols, basis, col_ref, row_ref, sci_ref, svar_ref, bad_ref):
    x = ag[slot, 0:POSITIONS]
    y = pltpu.roll(x, LANES // 2, 2)
    lane = lax.broadcasted_iota(jnp.int32, y.shape, 2)
    block = lax.broadcasted_iota(jnp.int32, y.shape, 1)
    before = jnp.where(block == 0, 0.0, pltpu.roll(y, 1, 1))
    after = jnp.where(block == NBLOCKS - 1, 0.0, pltpu.roll(y, NBLOCKS - 1, 1))
    low = lane < LANES // 2
    left = jnp.where(low, before, y).reshape(POSITIONS * NBLOCKS, LANES)
    right = jnp.where(low, y, after).reshape(POSITIONS * NBLOCKS, LANES)
    window = jnp.concatenate([left, right], axis=1)
    for k in range(NPROF):
        cols[k * POSITIONS * NBLOCKS : (k + 1) * POSITIONS * NBLOCKS, :] = jnp.dot(
            window,
            col_ref[:, k * LANES : (k + 1) * LANES],
            precision=lax.Precision.HIGHEST,
            preferred_element_type=jnp.float32,
        )

    def one_block(b, total):
        at = pl.multiple_of(b * LANES, LANES)
        c = jnp.concatenate(
            [
                cols[pl.ds(k * POSITIONS * NBLOCKS + b, POSITIONS, stride=NBLOCKS), :]
                for k in range(NPROF)
            ],
            axis=1,
        )
        high = rounded(c)
        rest = c - high
        mid = rounded(rest)
        low = rest - mid
        stacked = jnp.concatenate([high, mid, low, high, mid, high], axis=0).astype(jnp.bfloat16)
        d = jnp.dot(row_ref[...], stacked, preferred_element_type=jnp.float32)
        science = sci_ref[step, :, pl.ds(at, LANES)]
        usable = (1 - bad_ref[step, :, pl.ds(at, LANES)]).astype(jnp.float32)
        tile_var = ag_flat[pl.ds((slot * 56 + VAR_AT) * NBLOCKS + b, ROWS, stride=NBLOCKS), :]
        weight = usable / (svar_ref[step, :, pl.ds(at, LANES)] + tile_var)
        spread = jnp.broadcast_to(weight[:, None, :], (ROWS, 8, LANES)).reshape(ROWS * 8, LANES)
        sci_spread = jnp.broadcast_to(science[:, None, :], (ROWS, 8, LANES)).reshape(ROWS * 8, LANES)
        place = lax.broadcasted_iota(jnp.int32, (ROWS * 8, LANES), 0) & 7
        first = jnp.where(place == SCI, sci_spread, d[:, 0:LANES])
        parts = [first] + [d[:, k * LANES : (k + 1) * LANES] for k in range(1, NPROF)]
        for k in range(NPROF):
            basis[slot, b, :, k * LANES : (k + 1) * LANES] = parts[k]

        def arranged(pieces):
            return jnp.concatenate(
                [
                    jnp.concatenate([piece[h * 8 : h * 8 + 8] for piece in pieces], axis=0)
                    for h in range(ROWS)
                ],
                axis=1,
            )

        def two(pieces):
            highs = [rounded(piece) for piece in pieces]
            rests = [piece - h for piece, h in zip(pieces, highs)]
            return arranged(highs + rests).astype(jnp.bfloat16)

        right = two(parts)
        left = two([piece * spread for piece in parts])
        product = lax.dot_general(
            left, right, (((1,), (1,)), ((), ())), preferred_element_type=jnp.float32
        )
        return total + product

    total = lax.fori_loop(0, NBLOCKS, one_block, jnp.zeros((80, 80), jnp.float32))
    full = total[0:40, 0:40] + total[0:40, 40:80] + total[40:80, 0:40] + total[40:80, 40:80]
    return full


def solve(mats):
    row = lax.broadcasted_iota(jnp.int32, (40, LANES), 0)
    col = lax.broadcasted_iota(jnp.int32, (40, LANES), 1)
    mats = [m + jnp.where(row == col, RIDGE, 0.0) for m in mats]
    for k in range(NPROF):
        for l in range(NPROF):
            p = k * 8 + l
            for s in range(STEPS):
                m = mats[s]
                pivot = m[p : p + 1, :] / m[p : p + 1, p : p + 1]
                mats[s] = jnp.where(row == p, pivot, m - m[:, p : p + 1] * pivot)
    return [
        jnp.where(row == SCI, -1.0, jnp.broadcast_to(m[:, SCI : SCI + 1], (40, LANES)))
        for m in mats
    ]


def kernel(
    owners, temp_ref, sci_ref, svar_ref, bad_ref, col_ref, row_ref, out_ref,
    mine, recv1, send2, recv2, ag, red, cols, basis,
    ssem1, same_sem, cross_sem, ssem2, rsem2, static_send, static_recv, ssem3, rsem3, ssem4, rsem4,
):
    v = lax.axis_index("visit")
    p = lax.axis_index("patch")
    group = v // GROUP
    cls = v % GROUP

    def peer(t):
        return group * GROUP + t

    recv1[...] = jnp.zeros_like(recv1)
    flat = mine.reshape(2 * ROWS * NBLOCKS, LANES)
    for kind in range(2):
        for half in range(2):
            for b in range(NBLOCKS):
                flat[pl.ds((kind * ROWS + half * 8) * NBLOCKS + b, 8, stride=NBLOCKS), :] = temp_ref[
                    kind, half * 8 : half * 8 + 8, b * LANES : (b + 1) * LANES
                ]

    barrier = pltpu.get_barrier_semaphore()

    def greet(vv, pp):
        pl.semaphore_signal(barrier, inc=1, device_id=(vv, pp), device_id_type=MESH)

    for d in range(1, GROUP):
        greet(peer((cls + d) % GROUP), p)
    for d in range(1, NGROUPS):
        greet(((group + d) % NGROUPS) * GROUP + cls, p)
    for d in range(1, NPATCH):
        greet(v, (p + d) % NPATCH)

    @pl.when((cls < 2) & (p > 0))
    def _():
        for d in range(1, GROUP):
            greet(peer((cls + d) % GROUP), p - 1)

    @pl.when(((cls == 4) | (cls == 5)) & (p < NPATCH - 1))
    def _():
        for d in range(1, GROUP):
            greet(peer((cls + d) % GROUP), p + 1)

    below = jnp.where(p < NPATCH - 1, jnp.where(cls < 2, 1, 2), 0)
    above = jnp.where(p > 0, jnp.where((cls == 4) | (cls == 5), 1, 2), 0)
    pl.semaphore_wait(barrier, GROUP - 1 + NGROUPS - 1 + NPATCH - 1 + below + above)

    def first_copy(i):
        t, dp, at, n, to = PARTS[i]
        return pltpu.make_async_remote_copy(
            src_ref=mine.at[pl.ds(at, n)],
            dst_ref=recv1.at[pl.ds(cls * SLOT + to, n)],
            send_sem=ssem1.at[i],
            recv_sem=same_sem if dp == 0 else cross_sem,
            device_id=(peer(t), p + dp),
            device_id_type=MESH,
        )

    def sends(i):
        t, dp = PARTS[i][:2]
        if dp == 0:
            return cls != t
        return p < NPATCH - 1 if dp == 1 else p > 0

    for i in range(len(PARTS)):

        @pl.when(sends(i))
        def _(i=i):
            first_copy(i).start()

    for t, dp, at, n, to in PARTS:

        @pl.when(cls == t)
        def _(t=t, dp=dp, at=at, n=n, to=to):
            if dp == 0:
                recv1[pl.ds(t * SLOT + to, n)] = mine[pl.ds(at, n)]

    for t, dp, at, n, to in PARTS:
        if dp == 0:

            @pl.when(cls == t)
            def _(n=n):
                rows = recv1.at[pl.ds(0, (GROUP - 1) * n)]
                pltpu.make_async_copy(rows, rows, same_sem).wait()

        else:

            @pl.when((cls == t) & (p > 0 if dp == 1 else p < NPATCH - 1))
            def _(n=n):
                rows = recv1.at[pl.ds(0, GROUP * n)]
                pltpu.make_async_copy(rows, rows, cross_sem).wait()

    own = pl.ds(cls * SLOT, SLOT)
    fixed = pl.ds((FIXED % GROUP) * SLOT, SLOT)

    def static_copy(g):
        return pltpu.make_async_remote_copy(
            src_ref=recv1.at[fixed],
            dst_ref=ag.at[0, own],
            send_sem=static_send.at[g],
            recv_sem=static_recv,
            device_id=(g * GROUP + cls, p),
            device_id_type=MESH,
        )

    @pl.when(group == FIXED // GROUP)
    def _():
        for g in range(NGROUPS - 1):
            static_copy(g).start()
        ag[0, own] = recv1[fixed]

    other = owners[0] + owners[1] - FIXED
    chosen = recv1[pl.ds((other & 7) * SLOT, SLOT)]
    send2[...] = chosen
    recv2[pl.ds(group * SLOT, SLOT)] = chosen

    def second_copy(d):
        return pltpu.make_async_remote_copy(
            src_ref=send2,
            dst_ref=recv2.at[pl.ds(group * SLOT, SLOT)],
            send_sem=ssem2.at[d],
            recv_sem=rsem2.at[d],
            device_id=(((group + d) % NGROUPS) * GROUP + cls, p),
            device_id_type=MESH,
        )

    for d in (2, 1, 3):
        second_copy(d).start()

    def third_copy(slot, d):
        return pltpu.make_async_remote_copy(
            src_ref=ag.at[slot, own],
            dst_ref=ag.at[slot, own],
            send_sem=ssem3.at[slot, d],
            recv_sem=rsem3.at[slot],
            device_id=(peer((cls + d) % GROUP), p),
            device_id_type=MESH,
        )

    @pl.when(group != FIXED // GROUP)
    def _():
        pltpu.make_async_copy(ag.at[0, own], ag.at[0, own], static_recv).wait()

    for d in range(1, GROUP):
        third_copy(0, d).start()
    for d in range(1, NGROUPS):
        second_copy(d).wait_recv()
    ag[1, own] = recv2[pl.ds(((other >> 3) & 3) * SLOT, SLOT)]
    for d in range(1, GROUP):
        third_copy(1, d).start()

    ag_flat = ag.reshape(STEPS * 56 * NBLOCKS, LANES)
    fixed_step = jnp.where(owners[1] == FIXED, 1, 0)
    found = []
    for slot in range(STEPS):
        rows = ag.at[slot, pl.ds(0, (GROUP - 1) * SLOT)]
        pltpu.make_async_copy(rows, rows, rsem3.at[slot]).wait()
        step = fixed_step if slot == 0 else 1 - fixed_step
        found.append(
            normal_part(slot, step, ag, ag_flat, cols, basis, col_ref, row_ref, sci_ref, svar_ref, bad_ref)
        )
    wide = [jnp.concatenate([m, jnp.zeros((40, LANES - 40), jnp.float32)], axis=1) for m in found]
    red[p] = wide[0] + pltpu.roll(wide[1], 64, 1)

    def fourth_copy(d):
        return pltpu.make_async_remote_copy(
            src_ref=red.at[p],
            dst_ref=red.at[p],
            send_sem=ssem4.at[d],
            recv_sem=rsem4.at[d],
            device_id=(v, (p + d) % NPATCH),
            device_id_type=MESH,
        )

    for d in range(1, NPATCH):
        fourth_copy(d).start()
    for d in range(1, NPATCH):
        fourth_copy(d).wait_recv()
    total = red[0]
    for q in range(1, NPATCH):
        total = total + red[q]

    coefs = solve([total, pltpu.roll(total, 64, 1)])

    for step in range(STEPS):
        slot = jnp.where(fixed_step == step, 0, 1)
        coef = jnp.where(fixed_step == step, coefs[0], coefs[1])

        def one_block(b, carry, step=step, slot=slot, coef=coef):
            at = pl.multiple_of(b * LANES, LANES)
            sums = jnp.zeros((ROWS, 8, LANES), jnp.float32)
            for k in range(NPROF):
                d = basis[slot, b, :, k * LANES : (k + 1) * LANES].reshape(ROWS, 8, LANES)
                sums = sums + d * coef[k * 8 : k * 8 + 8][None]
            left = jnp.sum(sums, axis=1)
            usable = (1 - bad_ref[step, :, pl.ds(at, LANES)]).astype(jnp.float32)
            tile_var = ag_flat[pl.ds((slot * 56 + VAR_AT) * NBLOCKS + b, ROWS, stride=NBLOCKS), :]
            noise = svar_ref[step, :, pl.ds(at, LANES)] + tile_var
            out_ref[step, :, pl.ds(at, LANES)] = -(usable * left) / jnp.sqrt(noise)
            return carry

        lax.fori_loop(0, NBLOCKS, one_block, 0)

    for i in range(len(PARTS)):

        @pl.when(sends(i))
        def _(i=i):
            first_copy(i).wait_send()

    @pl.when(group == FIXED // GROUP)
    def _():
        for g in range(NGROUPS - 1):
            static_copy(g).wait_send()

    for d in range(1, NGROUPS):
        second_copy(d).wait_send()
    for slot in range(STEPS):
        for d in range(1, GROUP):
            third_copy(slot, d).wait_send()
    for d in range(1, NPATCH):
        fourth_copy(d).wait_send()


def shards(templates, owners, science, sci_var, bad_pixels):
    vmem = pl.BlockSpec(memory_space=pltpu.VMEM)
    row_shape = (NBLOCKS, LANES)
    dma = pltpu.SemaphoreType.DMA
    result = pl.pallas_call(
        kernel,
        out_shape=jax.ShapeDtypeStruct((STEPS, ROWS, NBLOCKS * LANES), jnp.float32),
        in_specs=[pl.BlockSpec(memory_space=pltpu.SMEM)] + [vmem] * 6,
        out_specs=vmem,
        scratch_shapes=[
            pltpu.VMEM((2 * ROWS, *row_shape), jnp.float32),
            pltpu.VMEM((GROUP * SLOT, *row_shape), jnp.float32),
            pltpu.VMEM((SLOT, *row_shape), jnp.float32),
            pltpu.VMEM((NGROUPS * SLOT, *row_shape), jnp.float32),
            pltpu.VMEM((STEPS, GROUP * SLOT, *row_shape), jnp.float32),
            pltpu.VMEM((NPATCH, 40, LANES), jnp.float32),
            pltpu.VMEM((NPROF * POSITIONS * NBLOCKS, LANES), jnp.float32),
            pltpu.VMEM((STEPS, NBLOCKS, ROWS * 8, NPROF * LANES), jnp.float32),
            dma((len(PARTS),)),
            dma,
            dma,
            dma((NGROUPS,)),
            dma((NGROUPS,)),
            dma((NGROUPS,)),
            dma,
            dma((STEPS, GROUP)),
            dma((STEPS,)),
            dma((NPATCH,)),
            dma((NPATCH,)),
        ],
        compiler_params=pltpu.CompilerParams(
            collective_id=0, has_side_effects=True, vmem_limit_bytes=32 * 1024 * 1024
        ),
        name="difference",
    )(
        owners,
        templates[0],
        science[:, 0],
        sci_var[:, 0],
        bad_pixels[:, 0],
        jnp.asarray(column_table()),
        jnp.asarray(row_table()),
    )
    return result[:, None]


def solution(mesh):
    return jax.shard_map(
        shards,
        mesh=mesh,
        in_specs=(
            P("visit", None, "patch", None),
            P(),
            P(None, "visit", "patch", None),
            P(None, "visit", "patch", None),
            P(None, "visit", "patch", None),
        ),
        out_specs=P(None, "visit", "patch", None),
        check_vma=False,
    )
```

time: 430 us -> 65.4 us (0.15)
  the two profiles are of different devices: /device:TPU:4 before, /device:TPU:1 now
where the time goes in v1:
time: 65.4 us; the launch traced here: 65.2 us
  Pallas kernels  58.3 us (89%)
  local copies, waits for them, and re-layouts  6.85 us (10%)
    pallas_call x1, Pallas kernels, shards(): pl.pallas_call(kernel, out_shape=jax.ShapeDtypeStruct((STEPS, ROWS, NBLOC...  58.3 us
    unnamed x15, local copies, waits for them, and re-layouts  6.85 us

profile of v1, /device:TPU:1, one launch (start us, length us, event | category | flops | bytes accessed | tf_op | source)
XLA Modules:
  0.0 65.2 jit_solution(3861918220446922285)
XLA Ops:
  0.0 0.0 copy-start.6
  0.0 0.7 %copy-done.6 = s32[2]{0:T(128)S(1)} copy-done((s32[2]{0:T(128)S(1)}, s32[2]{0:T(128)}, u32[]{:S(2)}) %copy-start.6) | copy-done | bytes 32
  0.7 0.0 copy-start
  0.7 1.1 %copy-done = f32[256,640]{1,0:T(8,128)S(1)} copy-done((f32[256,640]{1,0:T(8,128)S(1)}, f32[256,640]{1,0:T(8,128)}, u32[]{:S(2)}) %copy-start) | copy-done | bytes 655384
  1.7 0.0 copy-start.1
  1.7 0.9 %copy-done.1 = f32[1,2,16,1024]{3,2,1,0:T(8,128)S(1)} copy-done((f32[1,2,16,1024]{3,2,1,0:T(8,128)S(1)}, f32[1,2,16,1024]{3,2,1,0:T(8,128)}, u32[]{:S(2)}) %copy-start.1) | copy-done | bytes 131096
  2.6 0.0 copy-start.2
  2.7 0.9 %copy-done.2 = f32[2,1,16,1024]{3,2,1,0:T(8,128)S(1)} copy-done((f32[2,1,16,1024]{3,2,1,0:T(8,128)S(1)}, f32[2,1,16,1024]{3,2,1,0:T(8,128)}, u32[]{:S(2)}) %copy-start.2) | copy-done | bytes 131096
  3.6 0.0 copy-start.3
  3.6 0.9 %copy-done.3 = f32[2,1,16,1024]{3,2,1,0:T(8,128)S(1)} copy-done((f32[2,1,16,1024]{3,2,1,0:T(8,128)S(1)}, f32[2,1,16,1024]{3,2,1,0:T(8,128)}, u32[]{:S(2)}) %copy-start.3) | copy-done | bytes 131096
  4.5 0.0 copy-start.4
  4.5 0.9 %copy-done.4 = s32[2,1,16,1024]{3,2,1,0:T(8,128)S(1)} copy-done((s32[2,1,16,1024]{3,2,1,0:T(8,128)S(1)}, s32[2,1,16,1024]{3,2,1,0:T(8,128)}, u32[]{:S(2)}) %copy-start.4) | copy-done | bytes 131096
  5.4 0.0 copy-start.5
  5.4 0.8 %copy-done.5 = bf16[128,240]{1,0:T(8,128)(2,1)S(1)} copy-done((bf16[128,240]{1,0:T(8,128)(2,1)S(1)}, bf16[128,240]{1,0:T(8,128)(2,1)}, u32[]{:S(2)}) %copy-start.5) | copy-done | bytes 61464
  6.2 58.3 %difference.1 = f32[2,16,1024]{2,1,0:T(8,128)S(1)} custom-call(s32[2]{0:T(128)S(1)} %copy-done.6, f32[2,16,1024]{2,1,0:T(8,128)S(1)} %bitcast.8, f32[2,16,1024]{2,1,0:T(8,128)S(1)} %bitcast.9, f32[2,16,1024]{2,1,0:T(8,128)S(1)} %bitcast.10, s32[2,16,1024]{2,1,0:T(8,128)S(1)} %bitcast.11, f32[256,640]{1,0:T(8,128)S(1)} %copy-done, bf16[128,240]{1,0:T(8,128)(2,1)S(1)} %copy-done.5), custom_call_target="tpu_custom_call" | custom-call | tf_op jit(solution)/shard_map/difference/pallas_call | solution.py:411
  64.5 0.7 %copy.10 = f32[2,1,16,1024]{3,2,1,0:T(8,128)} copy(f32[2,1,16,1024]{3,2,1,0:T(8,128)S(1)} %bitcast.7) | data formatting | bytes 262144
Async XLA Ops:
  0.0 0.7 %copy-start.6 = (s32[2]{0:T(128)S(1)}, s32[2]{0:T(128)}, u32[]{:S(2)}) copy-start(s32[2]{0:T(128)} %owners.1) | copy-start | bytes 28
  0.7 1.1 %copy-start = (f32[256,640]{1,0:T(8,128)S(1)}, f32[256,640]{1,0:T(8,128)}, u32[]{:S(2)}) copy-start(f32[256,640]{1,0:T(8,128)} %constant.4.clone.col_ref) | copy-start | bytes 1966084
  1.7 0.9 %copy-start.1 = (f32[1,2,16,1024]{3,2,1,0:T(8,128)S(1)}, f32[1,2,16,1024]{3,2,1,0:T(8,128)}, u32[]{:S(2)}) copy-start(f32[1,2,16,1024]{3,2,1,0:T(8,128)} %param.7) | copy-start | bytes 393220
  2.6 0.9 %copy-start.2 = (f32[2,1,16,1024]{3,2,1,0:T(8,128)S(1)}, f32[2,1,16,1024]{3,2,1,0:T(8,128)}, u32[]{:S(2)}) copy-start(f32[2,1,16,1024]{3,2,1,0:T(8,128)} %param.9) | copy-start | bytes 393220
  3.6 0.9 %copy-start.3 = (f32[2,1,16,1024]{3,2,1,0:T(8,128)S(1)}, f32[2,1,16,1024]{3,2,1,0:T(8,128)}, u32[]{:S(2)}) copy-start(f32[2,1,16,1024]{3,2,1,0:T(8,128)} %param.10) | copy-start | bytes 393220
  4.5 0.9 %copy-start.4 = (s32[2,1,16,1024]{3,2,1,0:T(8,128)S(1)}, s32[2,1,16,1024]{3,2,1,0:T(8,128)}, u32[]{:S(2)}) copy-start(s32[2,1,16,1024]{3,2,1,0:T(8,128)} %param.11) | copy-start | bytes 393220
  5.4 0.8 %copy-start.5 = (bf16[128,240]{1,0:T(8,128)(2,1)S(1)}, bf16[128,240]{1,0:T(8,128)(2,1)}, u32[]{:S(2)}) copy-start(bf16[128,240]{1,0:T(8,128)(2,1)} %constant.5.clone.row_ref) | copy-start | bytes 184324

commit v2 on v1

--- a/solution.py
+++ b/solution.py
@@ -65,7 +65,8 @@
         for n in range(LANES):
             first = n + LANES // 2 - RAD
             table[first : first + 2 * RAD + 1, k * LANES + n] = prof[k]
-    return table
+    high, mid, _ = split3(table)
+    return np.concatenate([high, mid], axis=1).astype(ml_dtypes.bfloat16)
 
 
 def split3(x):
@@ -102,19 +103,21 @@
     left = jnp.where(low, before, y).reshape(POSITIONS * NBLOCKS, LANES)
     right = jnp.where(low, y, after).reshape(POSITIONS * NBLOCKS, LANES)
     window = jnp.concatenate([left, right], axis=1)
+    height = POSITIONS * NBLOCKS
+    high = rounded(window)
+    both = jnp.concatenate([high, window - high], axis=0).astype(jnp.bfloat16)
     for k in range(NPROF):
-        cols[k * POSITIONS * NBLOCKS : (k + 1) * POSITIONS * NBLOCKS, :] = jnp.dot(
-            window,
-            col_ref[:, k * LANES : (k + 1) * LANES],
-            precision=lax.Precision.HIGHEST,
-            preferred_element_type=jnp.float32,
-        )
+        table = col_ref[:, k * LANES : (k + 1) * LANES]
+        rest = col_ref[:, (NPROF + k) * LANES : (NPROF + k + 1) * LANES]
+        main = jnp.dot(both, table, preferred_element_type=jnp.float32)
+        more = jnp.dot(both[0:height], rest, preferred_element_type=jnp.float32)
+        cols[k * height : (k + 1) * height, :] = main[0:height] + (main[height:] + more)
 
     def one_block(b, total):
         at = pl.multiple_of(b * LANES, LANES)
         c = jnp.concatenate(
             [
-                cols[pl.ds(k * POSITIONS * NBLOCKS + b, POSITIONS, stride=NBLOCKS), :]
+                cols[pl.ds(k * height + b, POSITIONS, stride=NBLOCKS), :]
                 for k in range(NPROF)
             ],
             axis=1,
@@ -125,15 +128,16 @@
         low = rest - mid
         stacked = jnp.concatenate([high, mid, low, high, mid, high], axis=0).astype(jnp.bfloat16)
         d = jnp.dot(row_ref[...], stacked, preferred_element_type=jnp.float32)
-        science = sci_ref[step, :, pl.ds(at, LANES)]
-        usable = (1 - bad_ref[step, :, pl.ds(at, LANES)]).astype(jnp.float32)
+        science = sci_ref[step, 0, :, pl.ds(at, LANES)]
+        usable = (1 - bad_ref[step, 0, :, pl.ds(at, LANES)]).astype(jnp.float32)
         tile_var = ag_flat[pl.ds((slot * 56 + VAR_AT) * NBLOCKS + b, ROWS, stride=NBLOCKS), :]
-        weight = usable / (svar_ref[step, :, pl.ds(at, LANES)] + tile_var)
-        spread = jnp.broadcast_to(weight[:, None, :], (ROWS, 8, LANES)).reshape(ROWS * 8, LANES)
+        scale = usable / jnp.sqrt(svar_ref[step, 0, :, pl.ds(at, LANES)] + tile_var)
+        spread = jnp.broadcast_to(scale[:, None, :], (ROWS, 8, LANES)).reshape(ROWS * 8, LANES)
         sci_spread = jnp.broadcast_to(science[:, None, :], (ROWS, 8, LANES)).reshape(ROWS * 8, LANES)
         place = lax.broadcasted_iota(jnp.int32, (ROWS * 8, LANES), 0) & 7
-        first = jnp.where(place == SCI, sci_spread, d[:, 0:LANES])
-        parts = [first] + [d[:, k * LANES : (k + 1) * LANES] for k in range(1, NPROF)]
+        parts = [d[:, k * LANES : (k + 1) * LANES] for k in range(NPROF)]
+        parts[0] = jnp.where(place == SCI, sci_spread, parts[0])
+        parts = [part * spread for part in parts]
         for k in range(NPROF):
             basis[slot, b, :, k * LANES : (k + 1) * LANES] = parts[k]
 
@@ -144,23 +148,39 @@
                     for h in range(ROWS)
                 ],
                 axis=1,
-            )
-
-        def two(pieces):
-            highs = [rounded(piece) for piece in pieces]
-            rests = [piece - h for piece, h in zip(pieces, highs)]
-            return arranged(highs + rests).astype(jnp.bfloat16)
-
-        right = two(parts)
-        left = two([piece * spread for piece in parts])
-        product = lax.dot_general(
-            left, right, (((1,), (1,)), ((), ())), preferred_element_type=jnp.float32
-        )
-        return total + product
-
-    total = lax.fori_loop(0, NBLOCKS, one_block, jnp.zeros((80, 80), jnp.float32))
-    full = total[0:40, 0:40] + total[0:40, 40:80] + total[40:80, 0:40] + total[40:80, 40:80]
-    return full
+            ).astype(jnp.bfloat16)
+
+        highs = [rounded(part) for part in parts]
+        rests = [part - h for part, h in zip(parts, highs)]
+        return total + lax.dot_general(
+            arranged(highs + rests),
+            arranged(highs),
+            (((1,), (1,)), ((), ())),
+            preferred_element_type=jnp.float32,
+        )
+
+    total = lax.fori_loop(0, NBLOCKS, one_block, jnp.zeros((80, 40), jnp.float32), unroll=4)
+    return total[0:40] + (total[40:80] + total[40:80].T)
+
+
+def packed(mat):
+    wide = jnp.concatenate([mat, jnp.zeros((40, LANES - 40), jnp.float32)], axis=1)
+    first = wide[0:8] + pltpu.roll(wide[8:16], 40, 1) + pltpu.roll(wide[16:24], 80, 1)
+    return jnp.concatenate([first, wide[24:32] + pltpu.roll(wide[32:40], 40, 1)], axis=0)
+
+
+def unpacked(tiles):
+    first, second = tiles[0:8], tiles[8:16]
+    return jnp.concatenate(
+        [
+            first,
+            pltpu.roll(first, LANES - 40, 1),
+            pltpu.roll(first, LANES - 80, 1),
+            second,
+            pltpu.roll(second, LANES - 40, 1),
+        ],
+        axis=0,
+    )
 
 
 def solve(mats):
@@ -181,7 +201,8 @@
 
 
 def kernel(
-    owners, temp_ref, sci_ref, svar_ref, bad_ref, col_ref, row_ref, out_ref,
+    owners, temp_hbm, sci_hbm, svar_hbm, bad_hbm, col_hbm, row_hbm, out_ref,
+    temp_ref, sci_ref, svar_ref, bad_ref, col_ref, row_ref, load_sem,
     mine, recv1, send2, recv2, ag, red, cols, basis,
     ssem1, same_sem, cross_sem, ssem2, rsem2, static_send, static_recv, ssem3, rsem3, ssem4, rsem4,
 ):
@@ -193,14 +214,23 @@
     def peer(t):
         return group * GROUP + t
 
+    loads = [
+        pltpu.make_async_copy(src, dst, load_sem.at[i])
+        for i, (src, dst) in enumerate(
+            (
+                (temp_hbm, temp_ref),
+                (col_hbm, col_ref),
+                (row_hbm, row_ref),
+                (svar_hbm, svar_ref),
+                (bad_hbm, bad_ref),
+                (sci_hbm, sci_ref),
+            )
+        )
+    ]
+    for load in loads:
+        load.start()
+
     recv1[...] = jnp.zeros_like(recv1)
-    flat = mine.reshape(2 * ROWS * NBLOCKS, LANES)
-    for kind in range(2):
-        for half in range(2):
-            for b in range(NBLOCKS):
-                flat[pl.ds((kind * ROWS + half * 8) * NBLOCKS + b, 8, stride=NBLOCKS), :] = temp_ref[
-                    kind, half * 8 : half * 8 + 8, b * LANES : (b + 1) * LANES
-                ]
 
     barrier = pltpu.get_barrier_semaphore()
 
@@ -226,6 +256,15 @@
 
     below = jnp.where(p < NPATCH - 1, jnp.where(cls < 2, 1, 2), 0)
     above = jnp.where(p > 0, jnp.where((cls == 4) | (cls == 5), 1, 2), 0)
+    loads[0].wait()
+    flat = mine.reshape(2 * ROWS * NBLOCKS, LANES)
+    for kind in range(2):
+        for half in range(2):
+            for b in range(NBLOCKS):
+                flat[pl.ds((kind * ROWS + half * 8) * NBLOCKS + b, 8, stride=NBLOCKS), :] = temp_ref[
+                    0, kind, half * 8 : half * 8 + 8, b * LANES : (b + 1) * LANES
+                ]
+
     pl.semaphore_wait(barrier, GROUP - 1 + NGROUPS - 1 + NPATCH - 1 + below + above)
 
     def first_copy(i):
@@ -334,36 +373,38 @@
 
     ag_flat = ag.reshape(STEPS * 56 * NBLOCKS, LANES)
     fixed_step = jnp.where(owners[1] == FIXED, 1, 0)
-    found = []
+    for load in loads[1:]:
+        load.wait()
+
+    def fourth_copy(slot, d):
+        return pltpu.make_async_remote_copy(
+            src_ref=red.at[slot, p],
+            dst_ref=red.at[slot, p],
+            send_sem=ssem4.at[slot, d],
+            recv_sem=rsem4.at[slot],
+            device_id=(v, (p + d) % NPATCH),
+            device_id_type=MESH,
+        )
+
     for slot in range(STEPS):
         rows = ag.at[slot, pl.ds(0, (GROUP - 1) * SLOT)]
         pltpu.make_async_copy(rows, rows, rsem3.at[slot]).wait()
         step = fixed_step if slot == 0 else 1 - fixed_step
-        found.append(
+        red[slot, p] = packed(
             normal_part(slot, step, ag, ag_flat, cols, basis, col_ref, row_ref, sci_ref, svar_ref, bad_ref)
         )
-    wide = [jnp.concatenate([m, jnp.zeros((40, LANES - 40), jnp.float32)], axis=1) for m in found]
-    red[p] = wide[0] + pltpu.roll(wide[1], 64, 1)
-
-    def fourth_copy(d):
-        return pltpu.make_async_remote_copy(
-            src_ref=red.at[p],
-            dst_ref=red.at[p],
-            send_sem=ssem4.at[d],
-            recv_sem=rsem4.at[d],
-            device_id=(v, (p + d) % NPATCH),
-            device_id_type=MESH,
-        )
-
-    for d in range(1, NPATCH):
-        fourth_copy(d).start()
-    for d in range(1, NPATCH):
-        fourth_copy(d).wait_recv()
-    total = red[0]
-    for q in range(1, NPATCH):
-        total = total + red[q]
-
-    coefs = solve([total, pltpu.roll(total, 64, 1)])
+        for d in range(1, NPATCH):
+            fourth_copy(slot, d).start()
+
+    mats = []
+    for slot in range(STEPS):
+        rows = red.at[slot, pl.ds(0, NPATCH - 1)]
+        pltpu.make_async_copy(rows, rows, rsem4.at[slot]).wait()
+        total = red[slot, 0]
+        for q in range(1, NPATCH):
+            total = total + red[slot, q]
+        mats.append(unpacked(total))
+    coefs = solve(mats)
 
     for step in range(STEPS):
         slot = jnp.where(fixed_step == step, 0, 1)
@@ -375,14 +416,10 @@
             for k in range(NPROF):
                 d = basis[slot, b, :, k * LANES : (k + 1) * LANES].reshape(ROWS, 8, LANES)
                 sums = sums + d * coef[k * 8 : k * 8 + 8][None]
-            left = jnp.sum(sums, axis=1)
-            usable = (1 - bad_ref[step, :, pl.ds(at, LANES)]).astype(jnp.float32)
-            tile_var = ag_flat[pl.ds((slot * 56 + VAR_AT) * NBLOCKS + b, ROWS, stride=NBLOCKS), :]
-            noise = svar_ref[step, :, pl.ds(at, LANES)] + tile_var
-            out_ref[step, :, pl.ds(at, LANES)] = -(usable * left) / jnp.sqrt(noise)
+            out_ref[step, 0, :, pl.ds(at, LANES)] = -jnp.sum(sums, axis=1)
             return carry
 
-        lax.fori_loop(0, NBLOCKS, one_block, 0)
+        lax.fori_loop(0, NBLOCKS, one_block, 0, unroll=4)
 
     for i in range(len(PARTS)):
 
@@ -400,26 +437,30 @@
     for slot in range(STEPS):
         for d in range(1, GROUP):
             third_copy(slot, d).wait_send()
-    for d in range(1, NPATCH):
-        fourth_copy(d).wait_send()
+        for d in range(1, NPATCH):
+            fourth_copy(slot, d).wait_send()
 
 
 def shards(templates, owners, science, sci_var, bad_pixels):
-    vmem = pl.BlockSpec(memory_space=pltpu.VMEM)
+    hbm = pl.BlockSpec(memory_space=pltpu.HBM)
     row_shape = (NBLOCKS, LANES)
     dma = pltpu.SemaphoreType.DMA
-    result = pl.pallas_call(
+    col_table, rows_table = jnp.asarray(column_table()), jnp.asarray(row_table())
+    operands = (templates, science, sci_var, bad_pixels, col_table, rows_table)
+    return pl.pallas_call(
         kernel,
-        out_shape=jax.ShapeDtypeStruct((STEPS, ROWS, NBLOCKS * LANES), jnp.float32),
-        in_specs=[pl.BlockSpec(memory_space=pltpu.SMEM)] + [vmem] * 6,
-        out_specs=vmem,
-        scratch_shapes=[
+        out_shape=jax.ShapeDtypeStruct(science.shape, jnp.float32),
+        in_specs=[pl.BlockSpec(memory_space=pltpu.SMEM)] + [hbm] * len(operands),
+        out_specs=pl.BlockSpec(memory_space=pltpu.VMEM),
+        scratch_shapes=[pltpu.VMEM(x.shape, x.dtype) for x in operands]
+        + [
+            dma((len(operands),)),
             pltpu.VMEM((2 * ROWS, *row_shape), jnp.float32),
             pltpu.VMEM((GROUP * SLOT, *row_shape), jnp.float32),
             pltpu.VMEM((SLOT, *row_shape), jnp.float32),
             pltpu.VMEM((NGROUPS * SLOT, *row_shape), jnp.float32),
             pltpu.VMEM((STEPS, GROUP * SLOT, *row_shape), jnp.float32),
-            pltpu.VMEM((NPATCH, 40, LANES), jnp.float32),
+            pltpu.VMEM((STEPS, NPATCH, 16, LANES), jnp.float32),
             pltpu.VMEM((NPROF * POSITIONS * NBLOCKS, LANES), jnp.float32),
             pltpu.VMEM((STEPS, NBLOCKS, ROWS * 8, NPROF * LANES), jnp.float32),
             dma((len(PARTS),)),
@@ -431,23 +472,14 @@
             dma,
             dma((STEPS, GROUP)),
             dma((STEPS,)),
-            dma((NPATCH,)),
-            dma((NPATCH,)),
+            dma((STEPS, NPATCH)),
+            dma((STEPS,)),
         ],
         compiler_params=pltpu.CompilerParams(
             collective_id=0, has_side_effects=True, vmem_limit_bytes=32 * 1024 * 1024
         ),
         name="difference",
-    )(
-        owners,
-        templates[0],
-        science[:, 0],
-        sci_var[:, 0],
-        bad_pixels[:, 0],
-        jnp.asarray(column_table()),
-        jnp.asarray(row_table()),
-    )
-    return result[:, None]
+    )(owners, *operands)
 
 
 def solution(mesh):

time: 65.4 us -> 61.3 us (0.937)
  Pallas kernels: 58.3 us -> 54.1 us
    pallas_call x1, Pallas kernels: 58.3 us -> 54.1 us  [shards(): pl.pallas_call(kernel, out_shape=jax.ShapeDtypeStruct(science.shape, jnp....]
where the time goes in v2:
time: 61.3 us; the launch traced here: 61 us
  Pallas kernels  54.1 us (88%)
  local copies, waits for them, and re-layouts  6.85 us (11%)
    pallas_call x1, Pallas kernels, shards(): pl.pallas_call(kernel, out_shape=jax.ShapeDtypeStruct(science.shape, jnp....  54.1 us
    unnamed x15, local copies, waits for them, and re-layouts  6.85 us

profile of v2, /device:TPU:1, one launch (start us, length us, event | category | flops | bytes accessed | tf_op | source)
XLA Modules:
  0.0 61.0 jit_solution(11030263440075566577)
XLA Ops:
  0.0 0.0 copy-start
  0.0 1.1 %copy-done = bf16[256,1280]{1,0:T(8,128)(2,1)S(1)} copy-done((bf16[256,1280]{1,0:T(8,128)(2,1)S(1)}, bf16[256,1280]{1,0:T(8,128)(2,1)}, u32[]{:S(2)}) %copy-start) | copy-done | bytes 655384
  1.1 0.0 copy-start.1
  1.1 0.9 %copy-done.1 = f32[1,2,16,1024]{3,2,1,0:T(8,128)S(1)} copy-done((f32[1,2,16,1024]{3,2,1,0:T(8,128)S(1)}, f32[1,2,16,1024]{3,2,1,0:T(8,128)}, u32[]{:S(2)}) %copy-start.1) | copy-done | bytes 131096
  2.0 0.0 copy-start.2
  2.0 0.9 %copy-done.2 = f32[2,1,16,1024]{3,2,1,0:T(8,128)S(1)} copy-done((f32[2,1,16,1024]{3,2,1,0:T(8,128)S(1)}, f32[2,1,16,1024]{3,2,1,0:T(8,128)}, u32[]{:S(2)}) %copy-start.2) | copy-done | bytes 131096
  2.9 0.0 copy-start.3
  2.9 0.9 %copy-done.3 = f32[2,1,16,1024]{3,2,1,0:T(8,128)S(1)} copy-done((f32[2,1,16,1024]{3,2,1,0:T(8,128)S(1)}, f32[2,1,16,1024]{3,2,1,0:T(8,128)}, u32[]{:S(2)}) %copy-start.3) | copy-done | bytes 131096
  3.8 0.0 copy-start.4
  3.8 0.9 %copy-done.4 = s32[2,1,16,1024]{3,2,1,0:T(8,128)S(1)} copy-done((s32[2,1,16,1024]{3,2,1,0:T(8,128)S(1)}, s32[2,1,16,1024]{3,2,1,0:T(8,128)}, u32[]{:S(2)}) %copy-start.4) | copy-done | bytes 131096
  4.7 0.0 copy-start.5
  4.7 0.8 %copy-done.5 = bf16[128,240]{1,0:T(8,128)(2,1)S(1)} copy-done((bf16[128,240]{1,0:T(8,128)(2,1)S(1)}, bf16[128,240]{1,0:T(8,128)(2,1)}, u32[]{:S(2)}) %copy-start.5) | copy-done | bytes 61464
  5.5 0.0 copy-start.6
  5.5 0.7 %copy-done.6 = s32[2]{0:T(128)S(1)} copy-done((s32[2]{0:T(128)S(1)}, s32[2]{0:T(128)}, u32[]{:S(2)}) %copy-start.6) | copy-done | bytes 32
  6.2 54.1 %difference.1 = f32[2,1,16,1024]{3,2,1,0:T(8,128)S(1)} custom-call(s32[2]{0:T(128)S(1)} %copy-done.6, f32[1,2,16,1024]{3,2,1,0:T(8,128)S(1)} %copy-done.1, f32[2,1,16,1024]{3,2,1,0:T(8,128)S(1)} %copy-done.2, f32[2,1,16,1024]{3,2,1,0:T(8,128)S(1)} %copy-done.3, s32[2,1,16,1024]{3,2,1,0:T(8,128)S(1)} %copy-done.4, bf16[256,1280]{1,0:T(8,128)(2,1)S(1)} %copy-done, ...), custom_call_target="tpu_custom_call" | custom-call | tf_op jit(solution)/shard_map/difference/pallas_call | solution.py:450
  60.3 0.7 %copy.9 = f32[2,1,16,1024]{3,2,1,0:T(8,128)} copy(f32[2,1,16,1024]{3,2,1,0:T(8,128)S(1)} %difference.1) | data formatting | bytes 262144
Async XLA Ops:
  0.0 1.1 %copy-start = (bf16[256,1280]{1,0:T(8,128)(2,1)S(1)}, bf16[256,1280]{1,0:T(8,128)(2,1)}, u32[]{:S(2)}) copy-start(bf16[256,1280]{1,0:T(8,128)(2,1)} %constant.4.clone.col_hbm) | copy-start | bytes 1966084
  1.1 0.9 %copy-start.1 = (f32[1,2,16,1024]{3,2,1,0:T(8,128)S(1)}, f32[1,2,16,1024]{3,2,1,0:T(8,128)}, u32[]{:S(2)}) copy-start(f32[1,2,16,1024]{3,2,1,0:T(8,128)} %temp_hbm.1) | copy-start | bytes 393220
  2.0 0.9 %copy-start.2 = (f32[2,1,16,1024]{3,2,1,0:T(8,128)S(1)}, f32[2,1,16,1024]{3,2,1,0:T(8,128)}, u32[]{:S(2)}) copy-start(f32[2,1,16,1024]{3,2,1,0:T(8,128)} %sci_hbm.1) | copy-start | bytes 393220
  2.9 0.9 %copy-start.3 = (f32[2,1,16,1024]{3,2,1,0:T(8,128)S(1)}, f32[2,1,16,1024]{3,2,1,0:T(8,128)}, u32[]{:S(2)}) copy-start(f32[2,1,16,1024]{3,2,1,0:T(8,128)} %svar_hbm.1) | copy-start | bytes 393220
  3.8 0.9 %copy-start.4 = (s32[2,1,16,1024]{3,2,1,0:T(8,128)S(1)}, s32[2,1,16,1024]{3,2,1,0:T(8,128)}, u32[]{:S(2)}) copy-start(s32[2,1,16,1024]{3,2,1,0:T(8,128)} %bad_hbm.1) | copy-start | bytes 393220
  4.7 0.8 %copy-start.5 = (bf16[128,240]{1,0:T(8,128)(2,1)S(1)}, bf16[128,240]{1,0:T(8,128)(2,1)}, u32[]{:S(2)}) copy-start(bf16[128,240]{1,0:T(8,128)(2,1)} %constant.5.clone.row_hbm) | copy-start | bytes 184324
  5.5 0.7 %copy-start.6 = (s32[2]{0:T(128)S(1)}, s32[2]{0:T(128)}, u32[]{:S(2)}) copy-start(s32[2]{0:T(128)} %owners.1) | copy-start | bytes 28

commit v3 on v2

--- a/solution.py
+++ b/solution.py
@@ -476,7 +476,7 @@
             dma((STEPS,)),
         ],
         compiler_params=pltpu.CompilerParams(
-            collective_id=0, has_side_effects=True, vmem_limit_bytes=32 * 1024 * 1024
+            collective_id=0, has_side_effects=True, vmem_limit_bytes=60 * 1024 * 1024
         ),
         name="difference",
     )(owners, *operands)

time: 61.3 us -> 55.7 us (0.909)
  local copies, waits for them, and re-layouts: 6.85 us -> 1.57 us
    unnamed x15 -> x1, local copies, waits for them, and re-layouts: 6.85 us -> 1.57 us
where the time goes in v3:
time: 55.7 us; the launch traced here: 55.5 us
  Pallas kernels  53.9 us (97%)
  local copies, waits for them, and re-layouts  1.57 us (3%)
    pallas_call x1, Pallas kernels, shards(): pl.pallas_call(kernel, out_shape=jax.ShapeDtypeStruct(science.shape, jnp....  53.9 us
    unnamed x1, local copies, waits for them, and re-layouts  1.57 us

profile of v3, /device:TPU:1, one launch (start us, length us, event | category | flops | bytes accessed | tf_op | source)
XLA Modules:
  0.0 55.5 jit_solution(7195555847659907558)
XLA Ops:
  0.0 53.9 %difference.1 = f32[2,1,16,1024]{3,2,1,0:T(8,128)} custom-call(s32[2]{0:T(128)} %owners.1, f32[1,2,16,1024]{3,2,1,0:T(8,128)} %temp_hbm.1, f32[2,1,16,1024]{3,2,1,0:T(8,128)} %sci_hbm.1, f32[2,1,16,1024]{3,2,1,0:T(8,128)} %svar_hbm.1, s32[2,1,16,1024]{3,2,1,0:T(8,128)} %bad_hbm.1, bf16[256,1280]{1,0:T(8,128)(2,1)} %constant.4.clone.col_hbm, ...), custom_call_target="tpu_custom_call" | custom-call | tf_op jit(solution)/shard_map/difference/pallas_call | solution.py:450
  53.9 1.6 %copy.9 = f32[2,1,16,1024]{3,2,1,0:T(8,128)} copy(f32[2,1,16,1024]{3,2,1,0:T(8,128)} %difference.1) | data formatting | bytes 262144

commit v4 on v3

--- a/solution.py
+++ b/solution.py
@@ -204,7 +204,7 @@
     owners, temp_hbm, sci_hbm, svar_hbm, bad_hbm, col_hbm, row_hbm, out_ref,
     temp_ref, sci_ref, svar_ref, bad_ref, col_ref, row_ref, load_sem,
     mine, recv1, send2, recv2, ag, red, cols, basis,
-    ssem1, same_sem, cross_sem, ssem2, rsem2, static_send, static_recv, ssem3, rsem3, ssem4, rsem4,
+    ssem1, same_sem, cross_sem, ssem2, rsem2, static_send, static_recv, ssem3, rsem3, ssem4, rsem4, passed,
 ):
     v = lax.axis_index("visit")
     p = lax.axis_index("patch")
@@ -239,7 +239,7 @@
 
     for d in range(1, GROUP):
         greet(peer((cls + d) % GROUP), p)
-    for d in range(1, NGROUPS):
+    for d in (1, 3):
         greet(((group + d) % NGROUPS) * GROUP + cls, p)
     for d in range(1, NPATCH):
         greet(v, (p + d) % NPATCH)
@@ -265,7 +265,14 @@
                     0, kind, half * 8 : half * 8 + 8, b * LANES : (b + 1) * LANES
                 ]
 
-    pl.semaphore_wait(barrier, GROUP - 1 + NGROUPS - 1 + NPATCH - 1 + below + above)
+    pl.semaphore_wait(barrier, GROUP - 1 + 2 + NPATCH - 1 + below + above)
+
+    pl.semaphore_signal(
+        passed,
+        inc=1,
+        device_id=(((group + 1) % NGROUPS) * GROUP + cls, p),
+        device_id_type=MESH,
+    )
 
     def first_copy(i):
         t, dp, at, n, to = PARTS[i]
@@ -327,7 +334,7 @@
 
     @pl.when(group == FIXED // GROUP)
     def _():
-        for g in range(NGROUPS - 1):
+        for g in (0, 2):
             static_copy(g).start()
         ag[0, own] = recv1[fixed]
 
@@ -346,8 +353,15 @@
             device_id_type=MESH,
         )
 
-    for d in (2, 1, 3):
-        second_copy(d).start()
+    second_copy(1).start()
+    second_copy(3).start()
+    pl.semaphore_wait(passed, 1)
+
+    @pl.when(group == FIXED // GROUP)
+    def _():
+        static_copy(1).start()
+
+    second_copy(2).start()
 
     def third_copy(slot, d):
         return pltpu.make_async_remote_copy(
@@ -474,6 +488,7 @@
             dma((STEPS,)),
             dma((STEPS, NPATCH)),
             dma((STEPS,)),
+            pltpu.SemaphoreType.REGULAR,
         ],
         compiler_params=pltpu.CompilerParams(
             collective_id=0, has_side_effects=True, vmem_limit_bytes=60 * 1024 * 1024

time: 55.7 us -> 55.6 us (level)
  no operation moved by 1% of the time
where the time goes in v4:
time: 55.6 us; the launch traced here: 55.4 us
  Pallas kernels  53.8 us (97%)
  local copies, waits for them, and re-layouts  1.57 us (3%)
    pallas_call x1, Pallas kernels, shards(): pl.pallas_call(kernel, out_shape=jax.ShapeDtypeStruct(science.shape, jnp....  53.8 us
    unnamed x1, local copies, waits for them, and re-layouts  1.57 us

profile of v4, /device:TPU:1, one launch (start us, length us, event | category | flops | bytes accessed | tf_op | source)
XLA Modules:
  0.0 55.4 jit_solution(4697134384247262011)
XLA Ops:
  0.0 53.8 %difference.1 = f32[2,1,16,1024]{3,2,1,0:T(8,128)} custom-call(s32[2]{0:T(128)} %owners.1, f32[1,2,16,1024]{3,2,1,0:T(8,128)} %temp_hbm.1, f32[2,1,16,1024]{3,2,1,0:T(8,128)} %sci_hbm.1, f32[2,1,16,1024]{3,2,1,0:T(8,128)} %svar_hbm.1, s32[2,1,16,1024]{3,2,1,0:T(8,128)} %bad_hbm.1, bf16[256,1280]{1,0:T(8,128)(2,1)} %constant.4.clone.col_hbm, ...), custom_call_target="tpu_custom_call" | custom-call | tf_op jit(solution)/shard_map/difference/pallas_call | solution.py:464
  53.9 1.6 %copy.9 = f32[2,1,16,1024]{3,2,1,0:T(8,128)} copy(f32[2,1,16,1024]{3,2,1,0:T(8,128)} %difference.1) | data formatting | bytes 262144

commit v5 on v4

--- a/solution.py
+++ b/solution.py
@@ -16,6 +16,7 @@
 
 GROUP = 8
 NGROUPS = 4
+DEPTHS = 16
 NPATCH = 16
 SLOT = 7
 FIXED = 31
@@ -36,6 +37,17 @@
     (5, 0, 16, 3, 4),
     (6, 0, 19, 7, 0),
     (7, 0, 26, 6, 0),
+)
+SPREAD = (
+    (2, 1, 0, 4),
+    (-2, 1, 4, 3),
+    (2, 0, 0, 4),
+    (-2, 0, 4, 3),
+    (1, 1, 0, 7),
+    (-1, 1, 0, 7),
+    (1, 0, 0, 7),
+    (-1, 0, 0, 7),
+    (0, 1, 0, 7),
 )
 VAR_AT = 39
 POSITIONS = 40
@@ -210,9 +222,15 @@
     p = lax.axis_index("patch")
     group = v // GROUP
     cls = v % GROUP
-
-    def peer(t):
-        return group * GROUP + t
+    depth = v // 2
+    side = v % 2
+    deep = cls // 2
+
+    def near(dz, dx):
+        return ((depth + dz + DEPTHS) % DEPTHS) * 2 + (side + dx) % 2
+
+    def holder(t):
+        return ((depth + (t // 2 - deep + 5) % 4 - 1 + DEPTHS) % DEPTHS) * 2 + t % 2
 
     loads = [
         pltpu.make_async_copy(src, dst, load_sem.at[i])
@@ -237,8 +255,10 @@
     def greet(vv, pp):
         pl.semaphore_signal(barrier, inc=1, device_id=(vv, pp), device_id_type=MESH)
 
-    for d in range(1, GROUP):
-        greet(peer((cls + d) % GROUP), p)
+    for dz in range(-2, 3):
+        for dx in range(2):
+            if (dz, dx) != (0, 0):
+                greet(near(dz, dx), p)
     for d in (1, 3):
         greet(((group + d) % NGROUPS) * GROUP + cls, p)
     for d in range(1, NPATCH):
@@ -246,13 +266,17 @@
 
     @pl.when((cls < 2) & (p > 0))
     def _():
-        for d in range(1, GROUP):
-            greet(peer((cls + d) % GROUP), p - 1)
+        for dz in range(-2, 2):
+            for dx in range(2):
+                if (dz, dx) != (0, 0):
+                    greet(near(dz, dx), p - 1)
 
     @pl.when(((cls == 4) | (cls == 5)) & (p < NPATCH - 1))
     def _():
-        for d in range(1, GROUP):
-            greet(peer((cls + d) % GROUP), p + 1)
+        for dz in range(-2, 2):
+            for dx in range(2):
+                if (dz, dx) != (0, 0):
+                    greet(near(dz, dx), p + 1)
 
     below = jnp.where(p < NPATCH - 1, jnp.where(cls < 2, 1, 2), 0)
     above = jnp.where(p > 0, jnp.where((cls == 4) | (cls == 5), 1, 2), 0)
@@ -265,7 +289,7 @@
                     0, kind, half * 8 : half * 8 + 8, b * LANES : (b + 1) * LANES
                 ]
 
-    pl.semaphore_wait(barrier, GROUP - 1 + 2 + NPATCH - 1 + below + above)
+    pl.semaphore_wait(barrier, 9 + 2 + NPATCH - 1 + below + above)
 
     pl.semaphore_signal(
         passed,
@@ -278,10 +302,10 @@
         t, dp, at, n, to = PARTS[i]
         return pltpu.make_async_remote_copy(
             src_ref=mine.at[pl.ds(at, n)],
-            dst_ref=recv1.at[pl.ds(cls * SLOT + to, n)],
+            dst_ref=recv1.at[pl.ds((((deep - t // 2 + 2) & 3) * 2 + side) * SLOT + to, n)],
             send_sem=ssem1.at[i],
             recv_sem=same_sem if dp == 0 else cross_sem,
-            device_id=(peer(t), p + dp),
+            device_id=(holder(t), p + dp),
             device_id_type=MESH,
         )
 
@@ -302,7 +326,7 @@
         @pl.when(cls == t)
         def _(t=t, dp=dp, at=at, n=n, to=to):
             if dp == 0:
-                recv1[pl.ds(t * SLOT + to, n)] = mine[pl.ds(at, n)]
+                recv1[pl.ds((4 + t % 2) * SLOT + to, n)] = mine[pl.ds(at, n)]
 
     for t, dp, at, n, to in PARTS:
         if dp == 0:
@@ -320,7 +344,9 @@
                 pltpu.make_async_copy(rows, rows, cross_sem).wait()
 
     own = pl.ds(cls * SLOT, SLOT)
-    fixed = pl.ds((FIXED % GROUP) * SLOT, SLOT)
+    fixed = pl.ds((((FIXED // 2 + 2 - deep) & 3) * 2 + FIXED % 2) * SLOT, SLOT)
+    fixed_group = ((FIXED // 2 + 2 - deep) & (DEPTHS - 1)) >> 2
+    from_fixed = group == fixed_group
 
     def static_copy(g):
         return pltpu.make_async_remote_copy(
@@ -328,18 +354,19 @@
             dst_ref=ag.at[0, own],
             send_sem=static_send.at[g],
             recv_sem=static_recv,
-            device_id=(g * GROUP + cls, p),
+            device_id=(((group + g) % NGROUPS) * GROUP + cls, p),
             device_id_type=MESH,
         )
 
-    @pl.when(group == FIXED // GROUP)
+    @pl.when(from_fixed)
     def _():
-        for g in (0, 2):
-            static_copy(g).start()
+        for d in (1, 3):
+            static_copy(d).start()
         ag[0, own] = recv1[fixed]
 
     other = owners[0] + owners[1] - FIXED
-    chosen = recv1[pl.ds((other & 7) * SLOT, SLOT)]
+    far = (other >> 1) + 2 - deep
+    chosen = recv1[pl.ds(((far & 3) * 2 + (other & 1)) * SLOT, SLOT)]
     send2[...] = chosen
     recv2[pl.ds(group * SLOT, SLOT)] = chosen
 
@@ -357,32 +384,34 @@
     second_copy(3).start()
     pl.semaphore_wait(passed, 1)
 
-    @pl.when(group == FIXED // GROUP)
+    @pl.when(from_fixed)
     def _():
-        static_copy(1).start()
+        static_copy(2).start()
 
     second_copy(2).start()
 
     def third_copy(slot, d):
+        dz, dx, at, n = SPREAD[d]
+        rows = pl.ds(cls * SLOT + at, n)
         return pltpu.make_async_remote_copy(
-            src_ref=ag.at[slot, own],
-            dst_ref=ag.at[slot, own],
+            src_ref=ag.at[slot, rows],
+            dst_ref=ag.at[slot, rows],
             send_sem=ssem3.at[slot, d],
             recv_sem=rsem3.at[slot],
-            device_id=(peer((cls + d) % GROUP), p),
+            device_id=(near(dz, dx), p),
             device_id_type=MESH,
         )
 
-    @pl.when(group != FIXED // GROUP)
+    @pl.when(group != fixed_group)
     def _():
         pltpu.make_async_copy(ag.at[0, own], ag.at[0, own], static_recv).wait()
 
-    for d in range(1, GROUP):
+    for d in range(len(SPREAD)):
         third_copy(0, d).start()
     for d in range(1, NGROUPS):
         second_copy(d).wait_recv()
-    ag[1, own] = recv2[pl.ds(((other >> 3) & 3) * SLOT, SLOT)]
-    for d in range(1, GROUP):
+    ag[1, own] = recv2[pl.ds(((far >> 2) & 3) * SLOT, SLOT)]
+    for d in range(len(SPREAD)):
         third_copy(1, d).start()
 
     ag_flat = ag.reshape(STEPS * 56 * NBLOCKS, LANES)
@@ -441,15 +470,15 @@
         def _(i=i):
             first_copy(i).wait_send()
 
-    @pl.when(group == FIXED // GROUP)
+    @pl.when(from_fixed)
     def _():
-        for g in range(NGROUPS - 1):
-            static_copy(g).wait_send()
+        for d in range(1, NGROUPS):
+            static_copy(d).wait_send()
 
     for d in range(1, NGROUPS):
         second_copy(d).wait_send()
     for slot in range(STEPS):
-        for d in range(1, GROUP):
+        for d in range(len(SPREAD)):
             third_copy(slot, d).wait_send()
         for d in range(1, NPATCH):
             fourth_copy(slot, d).wait_send()
@@ -484,7 +513,7 @@
             dma((NGROUPS,)),
             dma((NGROUPS,)),
             dma,
-            dma((STEPS, GROUP)),
+            dma((STEPS, len(SPREAD))),
             dma((STEPS,)),
             dma((STEPS, NPATCH)),
             dma((STEPS,)),

time: 55.6 us -> 51.2 us (0.921)
  Pallas kernels: 53.8 us -> 49.5 us
    pallas_call x1, Pallas kernels: 53.8 us -> 49.5 us  [shards(): pl.pallas_call(kernel, out_shape=jax.ShapeDtypeStruct(science.shape, jnp....]
where the time goes in v5:
time: 51.2 us; the launch traced here: 51.1 us
  Pallas kernels  49.5 us (97%)
  local copies, waits for them, and re-layouts  1.57 us (3%)
    pallas_call x1, Pallas kernels, shards(): pl.pallas_call(kernel, out_shape=jax.ShapeDtypeStruct(science.shape, jnp....  49.5 us
    unnamed x1, local copies, waits for them, and re-layouts  1.57 us

profile of v5, /device:TPU:1, one launch (start us, length us, event | category | flops | bytes accessed | tf_op | source)
XLA Modules:
  0.0 51.1 jit_solution(1522329907810624173)
XLA Ops:
  0.0 49.5 %difference.1 = f32[2,1,16,1024]{3,2,1,0:T(8,128)} custom-call(s32[2]{0:T(128)} %owners.1, f32[1,2,16,1024]{3,2,1,0:T(8,128)} %temp_hbm.1, f32[2,1,16,1024]{3,2,1,0:T(8,128)} %sci_hbm.1, f32[2,1,16,1024]{3,2,1,0:T(8,128)} %svar_hbm.1, s32[2,1,16,1024]{3,2,1,0:T(8,128)} %bad_hbm.1, bf16[256,1280]{1,0:T(8,128)(2,1)} %constant.4.clone.col_hbm, ...), custom_call_target="tpu_custom_call" | custom-call | tf_op jit(solution)/shard_map/difference/pallas_call | solution.py:493
  49.5 1.6 %copy.9 = f32[2,1,16,1024]{3,2,1,0:T(8,128)} copy(f32[2,1,16,1024]{3,2,1,0:T(8,128)} %difference.1) | data formatting | bytes 262144

commit v6 on v5

--- a/solution.py
+++ b/solution.py
@@ -96,8 +96,9 @@
         for l in range(NPROF):
             for a in range(2 * RAD + 1):
                 table[h * 8 + l, places[h + a]] = prof[l, a]
-    high, mid, low = split3(table)
-    return np.concatenate([high, high, high, mid, mid, low], axis=1).astype(ml_dtypes.bfloat16)
+    high, mid, _ = split3(table)
+    blank = np.zeros((ROWS * 8, 8), np.float32)
+    return np.concatenate([high, high, mid, blank], axis=1).astype(ml_dtypes.bfloat16)
 
 
 def rounded(x):
@@ -135,10 +136,8 @@
             axis=1,
         )
         high = rounded(c)
-        rest = c - high
-        mid = rounded(rest)
-        low = rest - mid
-        stacked = jnp.concatenate([high, mid, low, high, mid, high], axis=0).astype(jnp.bfloat16)
+        blank = jnp.zeros((8, NPROF * LANES), jnp.float32)
+        stacked = jnp.concatenate([high, c - high, high, blank], axis=0).astype(jnp.bfloat16)
         d = jnp.dot(row_ref[...], stacked, preferred_element_type=jnp.float32)
         science = sci_ref[step, 0, :, pl.ds(at, LANES)]
         usable = (1 - bad_ref[step, 0, :, pl.ds(at, LANES)]).astype(jnp.float32)
@@ -202,7 +201,7 @@
     for k in range(NPROF):
         for l in range(NPROF):
             p = k * 8 + l
-            for s in range(STEPS):
+            for s in range(len(mats)):
                 m = mats[s]
                 pivot = m[p : p + 1, :] / m[p : p + 1, p : p + 1]
                 mats[s] = jnp.where(row == p, pivot, m - m[:, p : p + 1] * pivot)
@@ -215,7 +214,7 @@
 def kernel(
     owners, temp_hbm, sci_hbm, svar_hbm, bad_hbm, col_hbm, row_hbm, out_ref,
     temp_ref, sci_ref, svar_ref, bad_ref, col_ref, row_ref, load_sem,
-    mine, recv1, send2, recv2, ag, red, cols, basis,
+    mine, recv1, send2, recv2, ag, red, cols, basis, fitted,
     ssem1, same_sem, cross_sem, ssem2, rsem2, static_send, static_recv, ssem3, rsem3, ssem4, rsem4, passed,
 ):
     v = lax.axis_index("visit")
@@ -374,8 +373,8 @@
         return pltpu.make_async_remote_copy(
             src_ref=send2,
             dst_ref=recv2.at[pl.ds(group * SLOT, SLOT)],
-            send_sem=ssem2.at[d],
-            recv_sem=rsem2.at[d],
+            send_sem=ssem2,
+            recv_sem=rsem2,
             device_id=(((group + d) % NGROUPS) * GROUP + cls, p),
             device_id_type=MESH,
         )
@@ -396,7 +395,7 @@
         return pltpu.make_async_remote_copy(
             src_ref=ag.at[slot, rows],
             dst_ref=ag.at[slot, rows],
-            send_sem=ssem3.at[slot, d],
+            send_sem=ssem3.at[slot],
             recv_sem=rsem3.at[slot],
             device_id=(near(dz, dx), p),
             device_id_type=MESH,
@@ -408,8 +407,8 @@
 
     for d in range(len(SPREAD)):
         third_copy(0, d).start()
-    for d in range(1, NGROUPS):
-        second_copy(d).wait_recv()
+    three = recv2.at[pl.ds(0, (NGROUPS - 1) * SLOT)]
+    pltpu.make_async_copy(three, three, rsem2).wait()
     ag[1, own] = recv2[pl.ds(((far >> 2) & 3) * SLOT, SLOT)]
     for d in range(len(SPREAD)):
         third_copy(1, d).start()
@@ -423,7 +422,7 @@
         return pltpu.make_async_remote_copy(
             src_ref=red.at[slot, p],
             dst_ref=red.at[slot, p],
-            send_sem=ssem4.at[slot, d],
+            send_sem=ssem4.at[slot],
             recv_sem=rsem4.at[slot],
             device_id=(v, (p + d) % NPATCH),
             device_id_type=MESH,
@@ -439,49 +438,57 @@
         for d in range(1, NPATCH):
             fourth_copy(slot, d).start()
 
-    mats = []
+    for i in range(len(PARTS)):
+
+        @pl.when(sends(i))
+        def _(i=i):
+            first_copy(i).wait_send()
+
+    @pl.when(from_fixed)
+    def _():
+        for d in range(1, NGROUPS):
+            static_copy(d).wait_send()
+
+    pltpu.make_async_copy(three, three, ssem2).wait()
     for slot in range(STEPS):
+        rows = ag.at[slot, pl.ds(0, (GROUP - 1) * SLOT)]
+        pltpu.make_async_copy(rows, rows, ssem3.at[slot]).wait()
+
+    def coefs(slot):
         rows = red.at[slot, pl.ds(0, NPATCH - 1)]
         pltpu.make_async_copy(rows, rows, rsem4.at[slot]).wait()
         total = red[slot, 0]
         for q in range(1, NPATCH):
             total = total + red[slot, q]
-        mats.append(unpacked(total))
-    coefs = solve(mats)
-
-    for step in range(STEPS):
-        slot = jnp.where(fixed_step == step, 0, 1)
-        coef = jnp.where(fixed_step == step, coefs[0], coefs[1])
-
-        def one_block(b, carry, step=step, slot=slot, coef=coef):
-            at = pl.multiple_of(b * LANES, LANES)
-            sums = jnp.zeros((ROWS, 8, LANES), jnp.float32)
-            for k in range(NPROF):
-                d = basis[slot, b, :, k * LANES : (k + 1) * LANES].reshape(ROWS, 8, LANES)
-                sums = sums + d * coef[k * 8 : k * 8 + 8][None]
-            out_ref[step, 0, :, pl.ds(at, LANES)] = -jnp.sum(sums, axis=1)
-            return carry
-
-        lax.fori_loop(0, NBLOCKS, one_block, 0, unroll=4)
-
-    for i in range(len(PARTS)):
-
-        @pl.when(sends(i))
-        def _(i=i):
-            first_copy(i).wait_send()
-
-    @pl.when(from_fixed)
-    def _():
-        for d in range(1, NGROUPS):
-            static_copy(d).wait_send()
-
-    for d in range(1, NGROUPS):
-        second_copy(d).wait_send()
+        return solve([unpacked(total)])[0]
+
+    def fit(slot, coef, b):
+        sums = jnp.zeros((ROWS, 8, LANES), jnp.float32)
+        for k in range(NPROF):
+            d = basis[slot, b, :, k * LANES : (k + 1) * LANES].reshape(ROWS, 8, LANES)
+            sums = sums + d * coef[k * 8 : k * 8 + 8][None]
+        return -jnp.sum(sums, axis=1)
+
+    coef0 = coefs(0)
+
+    def fixed_block(b, carry):
+        fitted[:, pl.ds(pl.multiple_of(b * LANES, LANES), LANES)] = fit(0, coef0, b)
+        return carry
+
+    lax.fori_loop(0, NBLOCKS, fixed_block, 0, unroll=4)
+    coef1 = coefs(1)
+
+    def other_block(b, carry):
+        at = pl.multiple_of(b * LANES, LANES)
+        ours, theirs = fitted[:, pl.ds(at, LANES)], fit(1, coef1, b)
+        for step in range(STEPS):
+            out_ref[step, 0, :, pl.ds(at, LANES)] = jnp.where(fixed_step == step, ours, theirs)
+        return carry
+
+    lax.fori_loop(0, NBLOCKS, other_block, 0, unroll=4)
     for slot in range(STEPS):
-        for d in range(len(SPREAD)):
-            third_copy(slot, d).wait_send()
-        for d in range(1, NPATCH):
-            fourth_copy(slot, d).wait_send()
+        rows = red.at[slot, pl.ds(0, NPATCH - 1)]
+        pltpu.make_async_copy(rows, rows, ssem4.at[slot]).wait()
 
 
 def shards(templates, owners, science, sci_var, bad_pixels):
@@ -506,16 +513,17 @@
             pltpu.VMEM((STEPS, NPATCH, 16, LANES), jnp.float32),
             pltpu.VMEM((NPROF * POSITIONS * NBLOCKS, LANES), jnp.float32),
             pltpu.VMEM((STEPS, NBLOCKS, ROWS * 8, NPROF * LANES), jnp.float32),
+            pltpu.VMEM((ROWS, NBLOCKS * LANES), jnp.float32),
             dma((len(PARTS),)),
             dma,
             dma,
-            dma((NGROUPS,)),
-            dma((NGROUPS,)),
+            dma,
+            dma,
             dma((NGROUPS,)),
             dma,
-            dma((STEPS, len(SPREAD))),
             dma((STEPS,)),
-            dma((STEPS, NPATCH)),
+            dma((STEPS,)),
+            dma((STEPS,)),
             dma((STEPS,)),
             pltpu.SemaphoreType.REGULAR,
         ],

time: 51.2 us -> 50.4 us (0.984)
  Pallas kernels: 49.5 us -> 48.7 us
    pallas_call x1, Pallas kernels: 49.5 us -> 48.7 us  [shards(): pl.pallas_call(kernel, out_shape=jax.ShapeDtypeStruct(science.shape, jnp....]
where the time goes in v6:
time: 50.4 us; the launch traced here: 50.3 us
  Pallas kernels  48.7 us (97%)
  local copies, waits for them, and re-layouts  1.57 us (3%)
    pallas_call x1, Pallas kernels, shards(): pl.pallas_call(kernel, out_shape=jax.ShapeDtypeStruct(science.shape, jnp....  48.7 us
    unnamed x1, local copies, waits for them, and re-layouts  1.57 us

profile of v6, /device:TPU:1, one launch (start us, length us, event | category | flops | bytes accessed | tf_op | source)
XLA Modules:
  0.0 50.3 jit_solution(14513976495788950955)
XLA Ops:
  0.0 48.7 %difference.1 = f32[2,1,16,1024]{3,2,1,0:T(8,128)} custom-call(s32[2]{0:T(128)} %owners.1, f32[1,2,16,1024]{3,2,1,0:T(8,128)} %temp_hbm.1, f32[2,1,16,1024]{3,2,1,0:T(8,128)} %sci_hbm.1, f32[2,1,16,1024]{3,2,1,0:T(8,128)} %svar_hbm.1, s32[2,1,16,1024]{3,2,1,0:T(8,128)} %bad_hbm.1, bf16[256,1280]{1,0:T(8,128)(2,1)} %constant.4.clone.col_hbm, ...), custom_call_target="tpu_custom_call" | custom-call | tf_op jit(solution)/shard_map/difference/pallas_call | solution.py:500
  48.7 1.6 %copy.9 = f32[2,1,16,1024]{3,2,1,0:T(8,128)} copy(f32[2,1,16,1024]{3,2,1,0:T(8,128)} %difference.1) | data formatting | bytes 262144

commit v7 on v6

--- a/solution.py
+++ b/solution.py
@@ -215,7 +215,7 @@
     owners, temp_hbm, sci_hbm, svar_hbm, bad_hbm, col_hbm, row_hbm, out_ref,
     temp_ref, sci_ref, svar_ref, bad_ref, col_ref, row_ref, load_sem,
     mine, recv1, send2, recv2, ag, red, cols, basis, fitted,
-    ssem1, same_sem, cross_sem, ssem2, rsem2, static_send, static_recv, ssem3, rsem3, ssem4, rsem4, passed,
+    ssem1, same_sem, cross_sem, ssem2, rsem2, static_send, static_recv, ssem3, rsem3, ssem4, rsem4, passed, known,
 ):
     v = lax.axis_index("visit")
     p = lax.axis_index("patch")
@@ -260,7 +260,7 @@
                 greet(near(dz, dx), p)
     for d in (1, 3):
         greet(((group + d) % NGROUPS) * GROUP + cls, p)
-    for d in range(1, NPATCH):
+    for d in (1, NPATCH - 1):
         greet(v, (p + d) % NPATCH)
 
     @pl.when((cls < 2) & (p > 0))
@@ -288,7 +288,7 @@
                     0, kind, half * 8 : half * 8 + 8, b * LANES : (b + 1) * LANES
                 ]
 
-    pl.semaphore_wait(barrier, 9 + 2 + NPATCH - 1 + below + above)
+    pl.semaphore_wait(barrier, 9 + 2 + 2 + below + above)
 
     pl.semaphore_signal(
         passed,
@@ -320,6 +320,14 @@
         def _(i=i):
             first_copy(i).start()
 
+    def spread_word(r):
+        for d in (1 << r, NPATCH - (1 << r)):
+            pl.semaphore_signal(
+                known.at[r], inc=1, device_id=(v, (p + d) % NPATCH), device_id_type=MESH
+            )
+
+    spread_word(0)
+
     for t, dp, at, n, to in PARTS:
 
         @pl.when(cls == t)
@@ -357,9 +365,11 @@
             device_id_type=MESH,
         )
 
+    pl.semaphore_wait(passed, 1)
+
     @pl.when(from_fixed)
     def _():
-        for d in (1, 3):
+        for d in (2, 1, 3):
             static_copy(d).start()
         ag[0, own] = recv1[fixed]
 
@@ -379,15 +389,10 @@
             device_id_type=MESH,
         )
 
-    second_copy(1).start()
-    second_copy(3).start()
-    pl.semaphore_wait(passed, 1)
-
-    @pl.when(from_fixed)
-    def _():
-        static_copy(2).start()
-
-    second_copy(2).start()
+    for d in (2, 1, 3):
+        second_copy(d).start()
+    pl.semaphore_wait(known.at[0], 2)
+    spread_word(1)
 
     def third_copy(slot, d):
         dz, dx, at, n = SPREAD[d]
@@ -412,6 +417,8 @@
     ag[1, own] = recv2[pl.ds(((far >> 2) & 3) * SLOT, SLOT)]
     for d in range(len(SPREAD)):
         third_copy(1, d).start()
+    pl.semaphore_wait(known.at[1], 2)
+    spread_word(2)
 
     ag_flat = ag.reshape(STEPS * 56 * NBLOCKS, LANES)
     fixed_step = jnp.where(owners[1] == FIXED, 1, 0)
@@ -435,6 +442,8 @@
         red[slot, p] = packed(
             normal_part(slot, step, ag, ag_flat, cols, basis, col_ref, row_ref, sci_ref, svar_ref, bad_ref)
         )
+        if slot == 0:
+            pl.semaphore_wait(known.at[2], 2)
         for d in range(1, NPATCH):
             fourth_copy(slot, d).start()
 
@@ -526,6 +535,7 @@
             dma((STEPS,)),
             dma((STEPS,)),
             pltpu.SemaphoreType.REGULAR,
+            pltpu.SemaphoreType.REGULAR((3,)),
         ],
         compiler_params=pltpu.CompilerParams(
             collective_id=0, has_side_effects=True, vmem_limit_bytes=60 * 1024 * 1024

time: 50.4 us -> 50.3 us (level)
  no operation moved by 1% of the time
where the time goes in v7:
time: 50.3 us; the launch traced here: 50.2 us
  Pallas kernels  48.6 us (97%)
  local copies, waits for them, and re-layouts  1.57 us (3%)
    pallas_call x1, Pallas kernels, shards(): pl.pallas_call(kernel, out_shape=jax.ShapeDtypeStruct(science.shape, jnp....  48.6 us
    unnamed x1, local copies, waits for them, and re-layouts  1.57 us

profile of v7, /device:TPU:1, one launch (start us, length us, event | category | flops | bytes accessed | tf_op | source)
XLA Modules:
  0.0 50.2 jit_solution(4773109329877827926)
XLA Ops:
  0.0 48.6 %difference.1 = f32[2,1,16,1024]{3,2,1,0:T(8,128)} custom-call(s32[2]{0:T(128)} %owners.1, f32[1,2,16,1024]{3,2,1,0:T(8,128)} %temp_hbm.1, f32[2,1,16,1024]{3,2,1,0:T(8,128)} %sci_hbm.1, f32[2,1,16,1024]{3,2,1,0:T(8,128)} %svar_hbm.1, s32[2,1,16,1024]{3,2,1,0:T(8,128)} %bad_hbm.1, bf16[256,1280]{1,0:T(8,128)(2,1)} %constant.4.clone.col_hbm, ...), custom_call_target="tpu_custom_call" | custom-call | tf_op jit(solution)/shard_map/difference/pallas_call | solution.py:509
  48.6 1.6 %copy.9 = f32[2,1,16,1024]{3,2,1,0:T(8,128)} copy(f32[2,1,16,1024]{3,2,1,0:T(8,128)} %difference.1) | data formatting | bytes 262144

commit v8 on v7

--- a/solution.py
+++ b/solution.py
@@ -199,12 +199,18 @@
     col = lax.broadcasted_iota(jnp.int32, (40, LANES), 1)
     mats = [m + jnp.where(row == col, RIDGE, 0.0) for m in mats]
     for k in range(NPROF):
-        for l in range(NPROF):
-            p = k * 8 + l
-            for s in range(len(mats)):
-                m = mats[s]
-                pivot = m[p : p + 1, :] / m[p : p + 1, p : p + 1]
-                mats[s] = jnp.where(row == p, pivot, m - m[:, p : p + 1] * pivot)
+        pivots = [k * 8 + l for l in range(NPROF)]
+        for s, m in enumerate(mats):
+            columns = [jnp.broadcast_to(m[:, p : p + 1], (40, LANES)) for p in pivots]
+            for i, p in enumerate(pivots):
+                ours = columns[i]
+                inverse = 1.0 / ours[p : p + 1]
+                pivot = m[p : p + 1] * inverse
+                m = jnp.where(row == p, pivot, m - ours * pivot)
+                for j in range(i + 1, NPROF):
+                    other = columns[j][p : p + 1] * inverse
+                    columns[j] = jnp.where(row == p, other, columns[j] - ours * other)
+            mats[s] = m
     return [
         jnp.where(row == SCI, -1.0, jnp.broadcast_to(m[:, SCI : SCI + 1], (40, LANES)))
         for m in mats

time: 50.3 us -> 48.9 us (0.972)
  Pallas kernels: 48.6 us -> 47.2 us
    pallas_call x1, Pallas kernels: 48.6 us -> 47.2 us  [shards(): pl.pallas_call(kernel, out_shape=jax.ShapeDtypeStruct(science.shape, jnp....]
where the time goes in v8:
time: 48.9 us; the launch traced here: 48.8 us
  Pallas kernels  47.2 us (97%)
  local copies, waits for them, and re-layouts  1.57 us (3%)
    pallas_call x1, Pallas kernels, shards(): pl.pallas_call(kernel, out_shape=jax.ShapeDtypeStruct(science.shape, jnp....  47.2 us
    unnamed x1, local copies, waits for them, and re-layouts  1.57 us

profile of v8, /device:TPU:1, one launch (start us, length us, event | category | flops | bytes accessed | tf_op | source)
XLA Modules:
  0.0 48.8 jit_solution(5658952609528327023)
XLA Ops:
  0.0 47.2 %difference.1 = f32[2,1,16,1024]{3,2,1,0:T(8,128)} custom-call(s32[2]{0:T(128)} %owners.1, f32[1,2,16,1024]{3,2,1,0:T(8,128)} %temp_hbm.1, f32[2,1,16,1024]{3,2,1,0:T(8,128)} %sci_hbm.1, f32[2,1,16,1024]{3,2,1,0:T(8,128)} %svar_hbm.1, s32[2,1,16,1024]{3,2,1,0:T(8,128)} %bad_hbm.1, bf16[256,1280]{1,0:T(8,128)(2,1)} %constant.4.clone.col_hbm, ...), custom_call_target="tpu_custom_call" | custom-call | tf_op jit(solution)/shard_map/difference/pallas_call | solution.py:515
  47.2 1.6 %copy.9 = f32[2,1,16,1024]{3,2,1,0:T(8,128)} copy(f32[2,1,16,1024]{3,2,1,0:T(8,128)} %difference.1) | data formatting | bytes 262144

commit v9 on v8

--- a/solution.py
+++ b/solution.py
@@ -450,7 +450,7 @@
         )
         if slot == 0:
             pl.semaphore_wait(known.at[2], 2)
-        for d in range(1, NPATCH):
+        for d in (12, 4, 13, 11, 5, 3, 10, 6, 14, 8, 9, 7, 2, 15, 1):
             fourth_copy(slot, d).start()
 
     for i in range(len(PARTS)):

time: 48.9 us -> 48.9 us (level)
  no operation moved by 1% of the time
where the time goes in v9:
time: 48.9 us; the launch traced here: 48.8 us
  Pallas kernels  47.2 us (97%)
  local copies, waits for them, and re-layouts  1.57 us (3%)
    pallas_call x1, Pallas kernels, shards(): pl.pallas_call(kernel, out_shape=jax.ShapeDtypeStruct(science.shape, jnp....  47.2 us
    unnamed x1, local copies, waits for them, and re-layouts  1.57 us

profile of v9, /device:TPU:1, one launch (start us, length us, event | category | flops | bytes accessed | tf_op | source)
XLA Modules:
  0.0 48.8 jit_solution(16858351195261686173)
XLA Ops:
  0.0 47.2 %difference.1 = f32[2,1,16,1024]{3,2,1,0:T(8,128)} custom-call(s32[2]{0:T(128)} %owners.1, f32[1,2,16,1024]{3,2,1,0:T(8,128)} %temp_hbm.1, f32[2,1,16,1024]{3,2,1,0:T(8,128)} %sci_hbm.1, f32[2,1,16,1024]{3,2,1,0:T(8,128)} %svar_hbm.1, s32[2,1,16,1024]{3,2,1,0:T(8,128)} %bad_hbm.1, bf16[256,1280]{1,0:T(8,128)(2,1)} %constant.4.clone.col_hbm, ...), custom_call_target="tpu_custom_call" | custom-call | tf_op jit(solution)/shard_map/difference/pallas_call | solution.py:515
  47.2 1.6 %copy.9 = f32[2,1,16,1024]{3,2,1,0:T(8,128)} copy(f32[2,1,16,1024]{3,2,1,0:T(8,128)} %difference.1) | data formatting | bytes 262144

commit v10 on v8

--- a/solution.py
+++ b/solution.py
@@ -220,7 +220,7 @@
 def kernel(
     owners, temp_hbm, sci_hbm, svar_hbm, bad_hbm, col_hbm, row_hbm, out_ref,
     temp_ref, sci_ref, svar_ref, bad_ref, col_ref, row_ref, load_sem,
-    mine, recv1, send2, recv2, ag, red, cols, basis, fitted,
+    mine, recv1, recv2, ag, red, cols, basis, fitted,
     ssem1, same_sem, cross_sem, ssem2, rsem2, static_send, static_recv, ssem3, rsem3, ssem4, rsem4, passed, known,
 ):
     v = lax.axis_index("visit")
@@ -264,10 +264,6 @@
         for dx in range(2):
             if (dz, dx) != (0, 0):
                 greet(near(dz, dx), p)
-    for d in (1, 3):
-        greet(((group + d) % NGROUPS) * GROUP + cls, p)
-    for d in (1, NPATCH - 1):
-        greet(v, (p + d) % NPATCH)
 
     @pl.when((cls < 2) & (p > 0))
     def _():
@@ -283,10 +279,14 @@
                 if (dz, dx) != (0, 0):
                     greet(near(dz, dx), p + 1)
 
+    for d in (1, 3):
+        greet(((group + d) % NGROUPS) * GROUP + cls, p)
+    for d in (1, NPATCH - 1):
+        greet(v, (p + d) % NPATCH)
     below = jnp.where(p < NPATCH - 1, jnp.where(cls < 2, 1, 2), 0)
     above = jnp.where(p > 0, jnp.where((cls == 4) | (cls == 5), 1, 2), 0)
     loads[0].wait()
-    flat = mine.reshape(2 * ROWS * NBLOCKS, LANES)
+    flat = mine.reshape((2 * ROWS + 1) * NBLOCKS, LANES)
     for kind in range(2):
         for half in range(2):
             for b in range(NBLOCKS):
@@ -382,12 +382,11 @@
     other = owners[0] + owners[1] - FIXED
     far = (other >> 1) + 2 - deep
     chosen = recv1[pl.ds(((far & 3) * 2 + (other & 1)) * SLOT, SLOT)]
-    send2[...] = chosen
     recv2[pl.ds(group * SLOT, SLOT)] = chosen
 
     def second_copy(d):
         return pltpu.make_async_remote_copy(
-            src_ref=send2,
+            src_ref=recv2.at[pl.ds(group * SLOT, SLOT)],
             dst_ref=recv2.at[pl.ds(group * SLOT, SLOT)],
             send_sem=ssem2,
             recv_sem=rsem2,
@@ -520,13 +519,12 @@
         scratch_shapes=[pltpu.VMEM(x.shape, x.dtype) for x in operands]
         + [
             dma((len(operands),)),
-            pltpu.VMEM((2 * ROWS, *row_shape), jnp.float32),
+            pltpu.VMEM((2 * ROWS + 1, *row_shape), jnp.float32),
             pltpu.VMEM((GROUP * SLOT, *row_shape), jnp.float32),
-            pltpu.VMEM((SLOT, *row_shape), jnp.float32),
             pltpu.VMEM((NGROUPS * SLOT, *row_shape), jnp.float32),
             pltpu.VMEM((STEPS, GROUP * SLOT, *row_shape), jnp.float32),
             pltpu.VMEM((STEPS, NPATCH, 16, LANES), jnp.float32),
-            pltpu.VMEM((NPROF * POSITIONS * NBLOCKS, LANES), jnp.float32),
+            pltpu.VMEM((NPROF * POSITIONS * NBLOCKS + 8, LANES), jnp.float32),
             pltpu.VMEM((STEPS, NBLOCKS, ROWS * 8, NPROF * LANES), jnp.float32),
             pltpu.VMEM((ROWS, NBLOCKS * LANES), jnp.float32),
             dma((len(PARTS),)),

time: 48.9 us -> 49.4 us (1.010)
  no operation moved by 1% of the time
where the time goes in v10:
time: 49.4 us; the launch traced here: 49.2 us
  Pallas kernels  47.6 us (96%)
  local copies, waits for them, and re-layouts  1.57 us (3%)
    pallas_call x1, Pallas kernels, shards(): pl.pallas_call(kernel, out_shape=jax.ShapeDtypeStruct(science.shape, jnp....  47.6 us
    unnamed x1, local copies, waits for them, and re-layouts  1.57 us

profile of v10, /device:TPU:1, one launch (start us, length us, event | category | flops | bytes accessed | tf_op | source)
XLA Modules:
  0.0 49.2 jit_solution(12259898248188755277)
XLA Ops:
  0.0 47.6 %difference.1 = f32[2,1,16,1024]{3,2,1,0:T(8,128)} custom-call(s32[2]{0:T(128)} %owners.1, f32[1,2,16,1024]{3,2,1,0:T(8,128)} %temp_hbm.1, f32[2,1,16,1024]{3,2,1,0:T(8,128)} %sci_hbm.1, f32[2,1,16,1024]{3,2,1,0:T(8,128)} %svar_hbm.1, s32[2,1,16,1024]{3,2,1,0:T(8,128)} %bad_hbm.1, bf16[256,1280]{1,0:T(8,128)(2,1)} %constant.4.clone.col_hbm, ...), custom_call_target="tpu_custom_call" | custom-call | tf_op jit(solution)/shard_map/difference/pallas_call | solution.py:514
  47.6 1.6 %copy.9 = f32[2,1,16,1024]{3,2,1,0:T(8,128)} copy(f32[2,1,16,1024]{3,2,1,0:T(8,128)} %difference.1) | data formatting | bytes 262144

commit v11 on v8

--- a/solution.py
+++ b/solution.py
@@ -260,12 +260,12 @@
     def greet(vv, pp):
         pl.semaphore_signal(barrier, inc=1, device_id=(vv, pp), device_id_type=MESH)
 
+    for d in (1, 3):
+        greet(((group + d) % NGROUPS) * GROUP + cls, p)
     for dz in range(-2, 3):
         for dx in range(2):
             if (dz, dx) != (0, 0):
                 greet(near(dz, dx), p)
-    for d in (1, 3):
-        greet(((group + d) % NGROUPS) * GROUP + cls, p)
     for d in (1, NPATCH - 1):
         greet(v, (p + d) % NPATCH)
 

time: 48.9 us -> 48.9 us (level)
  no operation moved by 1% of the time
where the time goes in v11:
time: 48.9 us; the launch traced here: 48.7 us
  Pallas kernels  47.2 us (97%)
  local copies, waits for them, and re-layouts  1.57 us (3%)
    pallas_call x1, Pallas kernels, shards(): pl.pallas_call(kernel, out_shape=jax.ShapeDtypeStruct(science.shape, jnp....  47.2 us
    unnamed x1, local copies, waits for them, and re-layouts  1.57 us

profile of v11, /device:TPU:1, one launch (start us, length us, event | category | flops | bytes accessed | tf_op | source)
XLA Modules:
  0.0 48.7 jit_solution(18173496244959413913)
XLA Ops:
  0.0 47.2 %difference.1 = f32[2,1,16,1024]{3,2,1,0:T(8,128)} custom-call(s32[2]{0:T(128)} %owners.1, f32[1,2,16,1024]{3,2,1,0:T(8,128)} %temp_hbm.1, f32[2,1,16,1024]{3,2,1,0:T(8,128)} %sci_hbm.1, f32[2,1,16,1024]{3,2,1,0:T(8,128)} %svar_hbm.1, s32[2,1,16,1024]{3,2,1,0:T(8,128)} %bad_hbm.1, bf16[256,1280]{1,0:T(8,128)(2,1)} %constant.4.clone.col_hbm, ...), custom_call_target="tpu_custom_call" | custom-call | tf_op jit(solution)/shard_map/difference/pallas_call | solution.py:515
  47.2 1.6 %copy.9 = f32[2,1,16,1024]{3,2,1,0:T(8,128)} copy(f32[2,1,16,1024]{3,2,1,0:T(8,128)} %difference.1) | data formatting | bytes 262144
